TPU v7x, 256 devices: a whole 4x4x8 slice. The times are simulated.
256 devices in a mesh: lat: 8 (over x_hi, y), lon: 32 (over x_lo, z, core).
Axes of the slice: x: 4 (x_hi: 2, x_lo: 2; x = x_hi * 2 + x_lo), y: 4, z: 8, core: 2. Of those that a mesh axis runs over, the one named last changes fastest.
Arguments:
- tracers: float32 [2, 3, 2048, 4096], P(None, None, 'lat', 'lon'), may hold values from -6 to 6
- east_courant: float32 [3, 2048, 4096], P(None, 'lat', 'lon'), may hold values from -0.45 to 0.45
- north_courant: float32 [3, 2048, 4096], P(None, 'lat', 'lon'), may hold values from -0.45 to 0.45
- east_kappa: float32 [3, 2048, 4096], P(None, 'lat', 'lon'), may hold values from 0.01 to 0.1
- north_kappa: float32 [3, 2048, 4096], P(None, 'lat', 'lon'), may hold values from 0.01 to 0.1
- ocean_mask: int32 [3, 2048, 4096], P(None, 'lat', 'lon'), may hold values 0 or 1
- fold_map: int32 [4096], P('lon'), may hold values from 0 to 4095, as said below
Outputs:
- updated: float32 [2, 3, 2048, 4096], P(None, None, 'lat', 'lon')
Inputs may be any that keep to these rules, and one draw needn't show every extreme that they name: fold_map[i] = (P - 1 - i) mod 4096 for every column i, with one pivot P that is a multiple of 128.
All inputs are finite; a program needn't handle non-finite values. No bound on the sum of `ocean_mask` on one device may be relied on, other than what follows from the above.
Results may differ from a plain program's by a relative error of at most 0.00002.
Values sent between devices are 32-bit elements; how exact they have to be, the bound alone decides.
No kernel may reach another device: no remote copies, remote signals or barrier semaphores. Data moves between devices by JAX's collectives and lax.ppermute only.
A program may use at most 64 MiB of HBM per device.

v0:
```python
import jax
import jax.numpy as jnp
from jax import lax
from jax.sharding import PartitionSpec as P

STEPS = 2


def extended(cells, sides, width, closed):
    for axis, dim in sides:
        count = lax.axis_size(axis)
        ends = count if closed else count - 1
        head = lax.slice_in_dim(cells, 0, width, axis=dim)
        tail = lax.slice_in_dim(cells, cells.shape[dim] - width, cells.shape[dim], axis=dim)
        cells = jnp.concatenate(
            [
                lax.ppermute(tail, axis, [(i, (i + 1) % count) for i in range(ends)]),
                cells,
                lax.ppermute(head, axis, [((i + 1) % count, i) for i in range(ends)]),
            ],
            axis=dim,
        )
    return cells


def face_flux(behind, center, forward, beyond, courant, diffusivity, opened):
    centered = 7.0 * (center + forward) - (behind + beyond)
    upwind = 3.0 * (forward - center) - (beyond - behind)
    return opened * (
        courant * centered / 12.0
        - jnp.abs(courant) * upwind / 12.0
        - diffusivity * (forward - center)
    )


def local(tracers, east_courant, north_courant, east_kappa, north_kappa, ocean_mask, fold_map):
    row_count = tracers.shape[2]
    col_count = tracers.shape[3]
    levels = ocean_mask.shape[0]
    ocean = ocean_mask.astype(jnp.float32)
    lat_index = lax.axis_index("lat")
    southern = lat_index == 0
    northern = lat_index == lax.axis_size("lat") - 1
    coefficients = jnp.concatenate(
        [east_courant, north_courant, east_kappa, north_kappa, ocean], axis=0
    )
    padded = extended(coefficients, (("lat", 1), ("lon", 2)), 1, True)

    def member(which):
        return padded[which * levels : (which + 1) * levels]

    inner_rows = slice(1, row_count + 1)
    east_c = member(0)[:, inner_rows, 1 : col_count + 1]
    east_cw = member(0)[:, inner_rows, 0:1]
    east_k = member(2)[:, inner_rows, 1 : col_count + 1]
    east_kw = member(2)[:, inner_rows, 0:1]
    flags = member(4)
    open_east = flags[:, inner_rows, 1 : col_count + 1] * flags[:, inner_rows, 2 : col_count + 2]
    open_west = flags[:, inner_rows, 0:1] * flags[:, inner_rows, 1:2]
    north_c = member(1)[:, 0 : row_count + 1, 1 : col_count + 1]
    north_k = member(3)[:, 0 : row_count + 1, 1 : col_count + 1]
    columns = flags[:, :, 1 : col_count + 1]
    lower = jnp.where(southern, 0.0, columns[:, 0:1])
    upper = jnp.where(northern, columns[:, row_count : row_count + 1], columns[:, row_count + 1 :])
    adjusted = jnp.concatenate([lower, columns[:, 1 : row_count + 1], upper], axis=1)
    open_north = adjusted[:, 0 : row_count + 1] * adjusted[:, 1 : row_count + 2]
    state = tracers * ocean
    for step_index in range(STEPS):
        top = jnp.stack([state[:, :, -1], state[:, :, -2]], axis=2)
        strip = jnp.concatenate([state[:, :, :, :2], state[:, :, :, -2:]], axis=3)
        edges = extended(strip, (("lon", 3),), 2, True)
        western = edges[:, :, :, 0:2]
        eastern = edges[:, :, :, 6:8]
        across = extended(state, (("lat", 2),), 2, False)
        piece = lax.all_gather(top, "lon", axis=3, tiled=True)
        inside = (fold_map >= 0) & (fold_map < piece.shape[3])
        picked = jnp.take(piece, jnp.clip(fold_map, 0, piece.shape[3] - 1), axis=3)
        folded = jnp.where(inside, picked, 0.0)
        across = across.at[:, :, row_count + 2 : row_count + 4].set(
            jnp.where(northern, folded, across[:, :, row_count + 2 : row_count + 4])
        )
        before_one = jnp.concatenate([western[:, :, :, 1:2], state[:, :, :, :-1]], axis=3)
        after_one = jnp.concatenate([state[:, :, :, 1:], eastern[:, :, :, 0:1]], axis=3)
        after_two = jnp.concatenate([state[:, :, :, 2:], eastern], axis=3)
        east_flux = face_flux(before_one, state, after_one, after_two, east_c, east_k, open_east)
        west_face = face_flux(
            western[:, :, :, 0:1],
            western[:, :, :, 1:2],
            state[:, :, :, 0:1],
            state[:, :, :, 1:2],
            east_cw,
            east_kw,
            open_west,
        )
        east_prior = jnp.concatenate([west_face, east_flux[:, :, :, :-1]], axis=3)
        north_flux = face_flux(
            across[:, :, 0 : row_count + 1],
            across[:, :, 1 : row_count + 2],
            across[:, :, 2 : row_count + 3],
            across[:, :, 3 : row_count + 4],
            north_c,
            north_k,
            open_north,
        )
        state = ocean * (
            state - (east_flux - east_prior) - (north_flux[:, :, 1:] - north_flux[:, :, :-1])
        )
    return state


def solution(mesh):
    in_specs = (
        P(None, None, "lat", "lon"),
        P(None, "lat", "lon"),
        P(None, "lat", "lon"),
        P(None, "lat", "lon"),
        P(None, "lat", "lon"),
        P(None, "lat", "lon"),
        P("lon"),
    )
    out_specs = P(None, None, "lat", "lon")
    return jax.shard_map(local, mesh=mesh, in_specs=in_specs, out_specs=out_specs, check_vma=False)
```

profile of v0, /device:TPU:4, one launch (start us, length us, event | category | flops | bytes accessed | tf_op | source)
XLA Modules:
  0.0 181.7 jit_solution(12865579225753868825)
XLA Ops:
  2.4 5.0 %collective-permute-start.7 = (f32[2,3,2,128]{3,2,1,0:T(2,128)S(1)}, f32[2,3,2,128]{3,2,1,0:T(2,128)S(1)}, u32[]{:S(2)}, u32[]{:S(2)}) collective-permute-start(f32[2,3,2,128]{3,2,1,0:T(2,128)S(1)} %get-tuple-element.54), channel_id=1, source_target_pairs={{32,0},{64,32},{96,64},{128,96},{160,128},{192,160},{224,192},{33,... | collective-permute-start | bytes 18440 | tf_op jit(solution)/shard_map/ppermute | solution.py:19
  7.4 1.9 %collective-permute-start.6 = (f32[2,3,2,128]{3,2,1,0:T(2,128)S(1)}, f32[2,3,2,128]{3,2,1,0:T(2,128)S(1)}, u32[]{:S(2)}, u32[]{:S(2)}) collective-permute-start(f32[2,3,2,128]{3,2,1,0:T(2,128)S(1)} %get-tuple-element.53), channel_id=1, source_target_pairs={{0,32},{32,64},{64,96},{96,128},{128,160},{160,192},{192,224},{1,3... | collective-permute-start | bytes 18440 | tf_op jit(solution)/shard_map/ppermute | solution.py:17
  11.7 5.7 %collective-permute-start.1 = (f32[15,1,128]{2,0,1:T(8,128)S(1)}, f32[15,1,128]{2,0,1:T(8,128)S(1)}, u32[]{:S(2)}, u32[]{:S(2)}) collective-permute-start(f32[15,1,128]{2,0,1:T(8,128)S(1)} %copy.213), channel_id=1, source_target_pairs={{32,0},{64,32},{96,64},{128,96},{160,128},{192,160},{224,192},{0,2... | collective-permute-start | bytes 23048 | tf_op jit(solution)/shard_map/ppermute | solution.py:19
  19.5 38.3 %all_gather.6 = f32[2,3,2,4096]{3,2,1,0:T(2,128)S(1)} all-gather(f32[2,3,2,128]{3,2,1,0:T(2,128)S(1)} %pad_maximum_fusion.14), channel_id=1, replica_groups=mesh['lat'=8,'lon'=32] {'lon'}, dimensions={3}, use_global_device_ids=true | all-gather | bytes 202752 | tf_op jit(solution)/shard_map/all_gather | solution.py:75
  58.9 8.0 %copy.230 = f32[2,3,2,4096]{1,2,3,0:T(2,128)} copy(f32[2,3,2,4096]{3,2,1,0:T(2,128)S(1)} %all_gather.6) | data formatting | bytes 393216 | tf_op jit(solution)/shard_map/all_gather | solution.py:75
  66.9 4.3 %gather_fusion = f32[128,2,3,2]{2,3,1,0:T(2,128)S(1)} fusion(f32[2,3,2,4096]{1,2,3,0:T(2,128)} %copy.230, s32[1024]{0:T(1024)S(1)} %pad_clamp_fusion), kind=kCustom, calls=%fused_computation.clone | custom fusion | bytes 12800 | tf_op jit(solution)/shard_map/jit(_take)/gather | solution.py:77
  72.0 2.1 %fusion.12 = (f32[3,257,128]{2,1,0:T(8,128)S(1)}, f32[3,257,128]{2,1,0:T(8,128)S(1)}, f32[3,257,128]{2,1,0:T(8,128)}) fusion(f32[15,256,128]{2,1,0:T(8,128)} %copy-done, f32[15,1,128]{2,1,0:T(1,128)S(1)} %copy.214), kind=kLoop, calls=%fused_computation.59 | loop fusion | flops 296064 | bytes 3158016 | tf_op jit(solution)/shard_map/abs | solution.py:31
  74.3 2.6 %fusion.13 = (f32[15,258,1]{2,1,0:T(8,128)}, f32[15,258,1]{2,1,0:T(8,128)}) fusion(f32[15,258,128]{2,1,0:T(8,128)S(1)} %pad_maximum_fusion), kind=kLoop, calls=%fused_computation.60 | loop fusion | bytes 61920 | tf_op jit(solution)/shard_map/slice | solution.py:14
  76.9 3.1 %copy.223 = f32[15,258,1]{1,0,2:T(8,128)} copy(f32[15,258,1]{2,1,0:T(8,128)} %get-tuple-element.34) | data formatting | bytes 30960 | tf_op jit(solution)/shard_map/slice | solution.py:14
  80.4 3.1 %copy.216 = f32[15,258,1]{1,0,2:T(8,128)} copy(f32[15,258,1]{2,1,0:T(8,128)} %get-tuple-element.35) | data formatting | bytes 30960 | tf_op jit(solution)/shard_map/slice | solution.py:13
  83.5 3.4 %collective-permute-start.2 = (f32[15,258,1]{1,0,2:T(8,128)}, f32[15,258,1]{1,0,2:T(8,128)}, u32[]{:S(2)}, u32[]{:S(2)}) collective-permute-start(f32[15,258,1]{1,0,2:T(8,128)} %copy.216), channel_id=1, source_target_pairs={{1,0},{2,1},{3,2},{4,3},{5,4},{6,5},{7,6},{8,7},{9,8},{10,9},{11,1... | collective-permute-start | bytes 46448 | tf_op jit(solution)/shard_map/ppermute | solution.py:19
  87.0 2.5 %subtract_multiply_fusion.1 = f32[2,3,257,128]{3,2,1,0:T(8,128)} fusion(f32[2,3,260,128]{3,2,1,0:T(8,128)S(1)} %fusion.11, f32[3,257,128]{2,1,0:T(8,128)} %get-tuple-element.36, f32[3,257,128]{2,1,0:T(8,128)S(1)} %get-tuple-element.30, f32[3,257,128]{2,1,0:T(8,128)S(1)} %get-tuple-element.31, f32[3,257,128]{2,1,0:T(8,128)S(1)} %maximum_multiply_fusion), kind=kLoop, calls=%fused_computation.6 | loop fusion | flops 3158016 | bytes 5526528 | tf_op jit(solution)/shard_map/mul | solution.py:29
  93.8 2.0 %copy.222 = f32[2,3,256,2]{3,2,1,0:T(8,128)} copy(f32[2,3,256,2]{2,3,1,0:T(2,128)} %copy-done.34) | data formatting | bytes 24576 | tf_op jit(solution)/shard_map/ppermute | solution.py:19
  99.5 2.7 %copy.217 = f32[15,258,1]{2,1,0:T(8,128)} copy(f32[15,258,1]{1,0,2:T(8,128)} %collective-permute-done.2) | data formatting | bytes 30960 | tf_op jit(solution)/shard_map/ppermute | solution.py:19
  102.2 1.6 fusion.7
  111.1 3.9 %collective-permute-start.8 = (f32[2,3,256,2]{2,3,1,0:T(2,128)S(1)}, f32[2,3,256,2]{2,3,1,0:T(2,128)S(1)}, u32[]{:S(2)}, u32[]{:S(2)}) collective-permute-start(f32[2,3,256,2]{2,3,1,0:T(2,128)S(1)} %copy.232), channel_id=1, source_target_pairs={{1,0},{2,1},{3,2},{4,3},{5,4},{6,5},{7,6},{8,7},{9,8},{10,9},{11,1... | collective-permute-start | bytes 36872 | tf_op jit(solution)/shard_map/ppermute | solution.py:19
  114.9 1.9 %collective-permute-start.10 = (f32[2,3,2,128]{3,2,1,0:T(2,128)S(1)}, f32[2,3,2,128]{3,2,1,0:T(2,128)S(1)}, u32[]{:S(2)}, u32[]{:S(2)}) collective-permute-start(f32[2,3,2,128]{3,2,1,0:T(2,128)S(1)} %get-tuple-element.45), channel_id=1, source_target_pairs={{0,32},{32,64},{64,96},{96,128},{128,160},{160,192},{192,224},{1,3... | collective-permute-start | bytes 18440 | tf_op jit(solution)/shard_map/ppermute | solution.py:17
  116.9 7.5 %collective-permute-start.11 = (f32[2,3,2,128]{3,2,1,0:T(2,128)S(1)}, f32[2,3,2,128]{3,2,1,0:T(2,128)S(1)}, u32[]{:S(2)}, u32[]{:S(2)}) collective-permute-start(f32[2,3,2,128]{3,2,1,0:T(2,128)S(1)} %get-tuple-element.46), channel_id=1, source_target_pairs={{32,0},{64,32},{96,64},{128,96},{160,128},{192,160},{224,192},{33,... | collective-permute-start | bytes 18440 | tf_op jit(solution)/shard_map/ppermute | solution.py:19
  124.4 30.9 %all_gather.7 = f32[2,3,2,4096]{3,2,1,0:T(2,128)S(1)} all-gather(f32[2,3,2,128]{3,2,1,0:T(2,128)S(1)} %pad_maximum_fusion.15), channel_id=1, replica_groups=mesh['lat'=8,'lon'=32] {'lon'}, dimensions={3}, use_global_device_ids=true | all-gather | bytes 202752 | tf_op jit(solution)/shard_map/all_gather | solution.py:75
  155.4 8.1 %copy.239 = f32[2,3,2,4096]{1,2,3,0:T(2,128)} copy(f32[2,3,2,4096]{3,2,1,0:T(2,128)S(1)} %all_gather.7) | data formatting | bytes 393216 | tf_op jit(solution)/shard_map/all_gather | solution.py:75
  163.4 4.5 %gather_fusion.1 = f32[128,2,3,2]{2,3,1,0:T(2,128)S(1)} fusion(f32[2,3,2,4096]{1,2,3,0:T(2,128)} %copy.239, s32[1024]{0:T(1024)} %copy-done.37), kind=kCustom, calls=%fused_computation.1.clone | custom fusion | bytes 12800 | tf_op jit(solution)/shard_map/jit(_take)/gather | solution.py:77
  168.2 1.7 subtract_multiply_fusion
  173.3 2.8 %subtract_multiply_fusion.2 = f32[2,3,256,1]{3,2,1,0:T(8,128)} fusion(f32[2,3,256,1]{3,2,1,0:T(8,128)} %copy.237, f32[2,3,256,1]{3,2,1,0:T(8,128)S(1)} %copy.242, f32[2,3,256,128]{3,2,1,0:T(8,128)S(1)} %fusion.3, f32[3,256]{1,0:T(4,128)S(1)} %copy-done.31, f32[3,256]{1,0:T(4,128)S(1)} %copy-done.29, f32[3,256]{1,0:T(4,128)S(1)} %copy-done.33, ...), kind=kLoop, calls=%fused_computation.23 | loop fusion | flops 24576 | bytes 43008 | tf_op jit(solution)/shard_map/mul | solution.py:29
  177.2 3.3 %subtract_multiply_fusion.3 = f32[2,3,256,128]{3,2,1,0:T(8,128)S(1)} fusion(f32[2,3,256,128]{3,2,1,0:T(8,128)S(1)} %fusion.3, f32[2,3,256,2]{3,2,1,0:T(8,128)} %copy.236, f32[2,3,256,126]{3,2,1,0:T(8,128)} %slice.377, f32[2,3,256,127]{3,2,1,0:T(8,128)} %get-tuple-element.40, f32[2,3,256,1]{3,2,1,0:T(8,128)S(1)} %copy.242, f32[2,3,256,1]{3,2,1,0:T(8,128)} %copy.233, ...), kind=kLoop, calls=%fused_computation.24 | loop fusion | flops 3735552 | bytes 5505024 | tf_op jit(solution)/shard_map/mul | solution.py:29
  (162 shorter events, 30.2 us)
Async XLA Ops:
  0.0 9.4 %copy-start.14 = (f32[3,256,128]{2,1,0:T(8,128)S(1)}, f32[3,256,128]{2,1,0:T(8,128)}, u32[]{:S(2)}) copy-start(f32[3,256,128]{2,1,0:T(8,128)} %param.14) | copy-start | bytes 1179652
  0.0 10.2 %copy-start.24 = (f32[3,256,128]{2,1,0:T(8,128)S(1)}, f32[3,256,128]{2,1,0:T(8,128)}, u32[]{:S(2)}) copy-start(f32[3,256,128]{2,1,0:T(8,128)} %param.15) | copy-start | bytes 1179652
  1.1 9.1 %copy-start.11 = (f32[3,256,128]{2,1,0:T(8,128)S(1)}, f32[3,256,128]{2,1,0:T(8,128)}, u32[]{:S(2)}) copy-start(f32[3,256,128]{2,1,0:T(8,128)} %param.16) | copy-start | bytes 1179652
  1.1 9.2 %copy-start.25 = (f32[3,256,128]{2,1,0:T(8,128)S(1)}, f32[3,256,128]{2,1,0:T(8,128)}, u32[]{:S(2)}) copy-start(f32[3,256,128]{2,1,0:T(8,128)} %param.17) | copy-start | bytes 1179652
  2.4 69.3 %collective-permute-start.7 = (f32[2,3,2,128]{3,2,1,0:T(2,128)S(1)}, f32[2,3,2,128]{3,2,1,0:T(2,128)S(1)}, u32[]{:S(2)}, u32[]{:S(2)}) collective-permute-start(f32[2,3,2,128]{3,2,1,0:T(2,128)S(1)} %get-tuple-element.54), channel_id=1, source_target_pairs={{32,0},{64,32},{96,64},{128,96},{160,128},{192,160},{224,192},{33,... | collective-permute-start | bytes 18440 | tf_op jit(solution)/shard_map/ppermute | solution.py:19
  7.4 64.3 %collective-permute-start.6 = (f32[2,3,2,128]{3,2,1,0:T(2,128)S(1)}, f32[2,3,2,128]{3,2,1,0:T(2,128)S(1)}, u32[]{:S(2)}, u32[]{:S(2)}) collective-permute-start(f32[2,3,2,128]{3,2,1,0:T(2,128)S(1)} %get-tuple-element.53), channel_id=1, source_target_pairs={{0,32},{32,64},{64,96},{96,128},{128,160},{160,192},{192,224},{1,3... | collective-permute-start | bytes 18440 | tf_op jit(solution)/shard_map/ppermute | solution.py:17
  11.7 60.2 %collective-permute-start.1 = (f32[15,1,128]{2,0,1:T(8,128)S(1)}, f32[15,1,128]{2,0,1:T(8,128)S(1)}, u32[]{:S(2)}, u32[]{:S(2)}) collective-permute-start(f32[15,1,128]{2,0,1:T(8,128)S(1)} %copy.213), channel_id=1, source_target_pairs={{32,0},{64,32},{96,64},{128,96},{160,128},{192,160},{224,192},{0,2... | collective-permute-start | bytes 23048 | tf_op jit(solution)/shard_map/ppermute | solution.py:19
  17.4 54.5 %collective-permute-start = (f32[15,1,128]{2,0,1:T(8,128)S(1)}, f32[15,1,128]{2,0,1:T(8,128)S(1)}, u32[]{:S(2)}, u32[]{:S(2)}) collective-permute-start(f32[15,1,128]{2,0,1:T(8,128)S(1)} %copy.212), channel_id=1, source_target_pairs={{0,32},{32,64},{64,96},{96,128},{128,160},{160,192},{192,224},{224... | collective-permute-start | bytes 23048 | tf_op jit(solution)/shard_map/ppermute | solution.py:17
  18.0 71.5 %collective-permute-start.4 = (f32[2,3,256,2]{2,3,1,0:T(2,128)S(1)}, f32[2,3,256,2]{2,3,1,0:T(2,128)S(1)}, u32[]{:S(2)}, u32[]{:S(2)}) collective-permute-start(f32[2,3,256,2]{2,3,1,0:T(2,128)S(1)} %copy.220), channel_id=1, source_target_pairs={{0,1},{1,2},{2,3},{3,4},{4,5},{5,6},{6,7},{7,8},{8,9},{9,10},{10,1... | collective-permute-start | bytes 36872 | tf_op jit(solution)/shard_map/ppermute | solution.py:17
  19.4 52.4 %copy-start.38 = (pred[128]{0:T(512)(128)(4,1)}, pred[128]{0:T(512)(128)(4,1)S(1)}, u32[]{:S(2)}) copy-start(pred[128]{0:T(512)(128)(4,1)S(1)} %get-tuple-element.32) | copy-start | bytes 388
  19.5 52.4 %copy-start.40 = (pred[128]{0:T(512)(128)(4,1)}, pred[128]{0:T(512)(128)(4,1)S(1)}, u32[]{:S(2)}) copy-start(pred[128]{0:T(512)(128)(4,1)S(1)} %get-tuple-element.65) | copy-start | bytes 388
  19.5 47.5 %copy-start.37 = (s32[1024]{0:T(1024)}, s32[1024]{0:T(1024)S(1)}, u32[]{:S(2)}) copy-start(s32[1024]{0:T(1024)S(1)} %pad_clamp_fusion) | copy-start | bytes 12292
  71.7 20.2 %collective-permute-start.3 = (f32[2,3,256,2]{2,3,1,0:T(2,128)S(1)}, f32[2,3,256,2]{2,3,1,0:T(2,128)S(1)}, u32[]{:S(2)}, u32[]{:S(2)}) collective-permute-start(f32[2,3,256,2]{2,3,1,0:T(2,128)S(1)} %copy.218), channel_id=1, source_target_pairs={{1,0},{2,1},{3,2},{4,3},{5,4},{6,5},{7,6},{8,7},{9,8},{10,9},{11,1... | collective-permute-start | bytes 36872 | tf_op jit(solution)/shard_map/ppermute | solution.py:19
  74.1 12.9 %copy-start.6 = (f32[3,257,128]{2,1,0:T(8,128)}, f32[3,257,128]{2,1,0:T(8,128)S(1)}, u32[]{:S(2)}) copy-start(f32[3,257,128]{2,1,0:T(8,128)S(1)} %get-tuple-element.30) | copy-start | bytes 1184260
  74.1 12.9 %copy-start.8 = (f32[3,257,128]{2,1,0:T(8,128)}, f32[3,257,128]{2,1,0:T(8,128)S(1)}, u32[]{:S(2)}) copy-start(f32[3,257,128]{2,1,0:T(8,128)S(1)} %get-tuple-element.31) | copy-start | bytes 1184260
  80.0 15.9 %collective-permute-start.5 = (f32[15,258,1]{1,0,2:T(8,128)}, f32[15,258,1]{1,0,2:T(8,128)}, u32[]{:S(2)}, u32[]{:S(2)}) collective-permute-start(f32[15,258,1]{1,0,2:T(8,128)} %copy.223), channel_id=1, source_target_pairs={{0,1},{1,2},{2,3},{3,4},{4,5},{5,6},{6,7},{7,8},{8,9},{9,10},{10,1... | collective-permute-start | bytes 46448 | tf_op jit(solution)/shard_map/ppermute | solution.py:17
  83.5 15.9 %collective-permute-start.2 = (f32[15,258,1]{1,0,2:T(8,128)}, f32[15,258,1]{1,0,2:T(8,128)}, u32[]{:S(2)}, u32[]{:S(2)}) collective-permute-start(f32[15,258,1]{1,0,2:T(8,128)} %copy.216), channel_id=1, source_target_pairs={{1,0},{2,1},{3,2},{4,3},{5,4},{6,5},{7,6},{8,7},{9,8},{10,9},{11,1... | collective-permute-start | bytes 46448 | tf_op jit(solution)/shard_map/ppermute | solution.py:19
  93.8 8.4 %copy-start.2 = (f32[15,256,128]{2,1,0:T(8,128)S(1)}, f32[15,256,128]{2,1,0:T(8,128)}, u32[]{:S(2)}) copy-start(f32[15,256,128]{2,1,0:T(8,128)} %copy-done) | copy-start | bytes 5898244
  110.7 59.2 %collective-permute-start.9 = (f32[2,3,256,2]{2,3,1,0:T(2,128)S(1)}, f32[2,3,256,2]{2,3,1,0:T(2,128)S(1)}, u32[]{:S(2)}, u32[]{:S(2)}) collective-permute-start(f32[2,3,256,2]{2,3,1,0:T(2,128)S(1)} %copy.234), channel_id=1, source_target_pairs={{0,1},{1,2},{2,3},{3,4},{4,5},{5,6},{6,7},{7,8},{8,9},{9,10},{10,1... | collective-permute-start | bytes 36872 | tf_op jit(solution)/shard_map/ppermute | solution.py:17
  111.1 60.4 %collective-permute-start.8 = (f32[2,3,256,2]{2,3,1,0:T(2,128)S(1)}, f32[2,3,256,2]{2,3,1,0:T(2,128)S(1)}, u32[]{:S(2)}, u32[]{:S(2)}) collective-permute-start(f32[2,3,256,2]{2,3,1,0:T(2,128)S(1)} %copy.232), channel_id=1, source_target_pairs={{1,0},{2,1},{3,2},{4,3},{5,4},{6,5},{7,6},{8,7},{9,8},{10,9},{11,1... | collective-permute-start | bytes 36872 | tf_op jit(solution)/shard_map/ppermute | solution.py:19
  114.9 53.2 %collective-permute-start.10 = (f32[2,3,2,128]{3,2,1,0:T(2,128)S(1)}, f32[2,3,2,128]{3,2,1,0:T(2,128)S(1)}, u32[]{:S(2)}, u32[]{:S(2)}) collective-permute-start(f32[2,3,2,128]{3,2,1,0:T(2,128)S(1)} %get-tuple-element.45), channel_id=1, source_target_pairs={{0,32},{32,64},{64,96},{96,128},{128,160},{160,192},{192,224},{1,3... | collective-permute-start | bytes 18440 | tf_op jit(solution)/shard_map/ppermute | solution.py:17
  116.9 51.2 %collective-permute-start.11 = (f32[2,3,2,128]{3,2,1,0:T(2,128)S(1)}, f32[2,3,2,128]{3,2,1,0:T(2,128)S(1)}, u32[]{:S(2)}, u32[]{:S(2)}) collective-permute-start(f32[2,3,2,128]{3,2,1,0:T(2,128)S(1)} %get-tuple-element.46), channel_id=1, source_target_pairs={{32,0},{64,32},{96,64},{128,96},{160,128},{192,160},{224,192},{33,... | collective-permute-start | bytes 18440 | tf_op jit(solution)/shard_map/ppermute | solution.py:19
  155.4 12.8 %copy-start.39 = (pred[128]{0:T(512)(128)(4,1)S(1)}, pred[128]{0:T(512)(128)(4,1)}, u32[]{:S(2)}) copy-start(pred[128]{0:T(512)(128)(4,1)} %copy-done.38) | copy-start | bytes 388
  155.4 12.8 %copy-start.41 = (pred[128]{0:T(512)(128)(4,1)S(1)}, pred[128]{0:T(512)(128)(4,1)}, u32[]{:S(2)}) copy-start(pred[128]{0:T(512)(128)(4,1)} %copy-done.40) | copy-start | bytes 388
  (31 other events, 71.4 us)
where the time goes:
time: 183 us; the launch traced here: 182 us
  blocking collectives  69.2 us (38%)
  local copies, waits for them, and re-layouts  58.5 us (32%)
  starting transfers between devices  30 us (16%)
  other arithmetic  23.2 us (13%)
    all_gather x2, blocking collectives, local(): piece = lax.all_gather(top, 'lon', axis=3, tiled=True)  69.2 us
    ppermute x6, starting transfers between devices, extended(): lax.ppermute(head, axis, [((i + 1) % count, i) for i in range(ends)])  25.6 us
    all_gather x2, local copies, waits for them, and re-layouts, local(): piece = lax.all_gather(top, 'lon', axis=3, tiled=True)  16.1 us
    mul x6, other arithmetic, face_flux(): opened * (courant * centered / 12.0 - jnp.abs(courant) * upwind / 12.0 -...  11.7 us
    gather x4, local copies, waits for them, and re-layouts, local(): picked = jnp.take(piece, jnp.clip(fold_map, 0, piece.shape[3] - 1), axis=3)  9.15 us
    unnamed x91, local copies, waits for them, and re-layouts  6 us
    ppermute x4, local copies, waits for them, and re-layouts, extended(): lax.ppermute(head, axis, [((i + 1) % count, i) for i in range(ends)])  5.89 us
    slice x5, local copies, waits for them, and re-layouts, extended(): lax.slice_in_dim(cells, cells.shape[dim] - width, cells.shape[dim], axis=...  5.7 us
  transfers between devices with their start and end apart: 12, of which 0 were waited for; matrix products, arithmetic and copies ran while one was open for 31% of the time, Pallas kernels for 0%

commit v1 on v0

v1 whole, which is shorter than its diff:
```python
import functools

import jax
import jax.numpy as jnp
from jax import lax
from jax.experimental import pallas as pl
from jax.experimental.pallas import tpu as pltpu
from jax.sharding import PartitionSpec as P

BOTH = ("lat", "lon")
LEV = 3
MEM = 6
ROWS = 256
BLOCKS = 8
GROUPS = 4
F32 = jnp.float32


def lanes():
    return lax.broadcasted_iota(jnp.int32, (8, 128), 1)


def roll(x, shift):
    shift = shift % 128
    return x if shift == 0 else pltpu.roll(x, shift, axis=1)


def face(courant, kappa):
    size = jnp.abs(courant)
    slope = 3.0 * size + kappa
    seven = 7.0 * courant
    return -(courant + size), seven + slope, seven - slope, size - courant


def weigh(ocean, east, west, north, south):
    ea, eb, ec, ed = face(*east)
    wa, wb, wc, wd = face(*west)
    na, nb, nc, nd = face(*north)
    sa, sb, sc, sd = face(*south)
    return (
        ocean * (1.0 + (wc - eb) + (sc - nb)),
        ocean * wa,
        ocean * (wb - ea),
        ocean * (wd - ec),
        -(ocean * ed),
        ocean * sa,
        ocean * (sb - na),
        ocean * (sd - nc),
        -(ocean * nd),
    )


def apply(w, q, sides, below2, below1, above1, above2, lane):
    west2 = roll(jnp.where(lane >= 126, sides, q), 2)
    west1 = roll(jnp.where(lane == 127, sides, q), 1)
    east1 = roll(jnp.where(lane == 0, sides, q), -1)
    east2 = roll(jnp.where(lane < 2, sides, q), -2)
    across = (w[1] * west2 + w[2] * west1) + (w[3] * east1 + w[4] * east2)
    along = (w[5] * below2 + w[6] * below1) + (w[7] * above1 + w[8] * above2)
    return w[0] * q + (across + along)


def place(kept, x, source, target, count, lane):
    moved = roll(x, target - source)
    if count == 1:
        here = lane == target
    else:
        here = (lane >= target) & (lane < target + count)
    return jnp.where(here, moved, kept)


def rows_of(i, g):
    return pl.ds(pl.multiple_of(i * 8, 8) + 64 * g, 8)


def pack_kernel(t_ref, ue_ref, un_ref, ke_ref, kn_ref, m_ref, a_ref, b_ref, e_ref, w_ref, nb, sb):
    lane = lanes()
    nb[...] = jnp.zeros((64, 128), F32)
    sb[...] = jnp.zeros((64, 128), F32)
    for lev in range(LEV):
        base = 24 + 12 * lev
        for out, lo, rows, faces in ((nb, ROWS - 8, slice(6, 8), slice(5, 7)), (sb, 0, slice(0, 2), slice(0, 2))):
            tile = pl.ds(lo, 8)
            ocean = m_ref[lev, tile].astype(F32)
            beside = jnp.where(lane == 127, 1.0, roll(ocean, -1))
            up = slice(faces.start + 1, faces.stop + 1)
            shut = ocean[faces] * ocean[up]
            un = un_ref[lev, tile] * (1.0 / 12.0)
            kn = kn_ref[lev, tile]
            out[base : base + 2] = un[faces] * shut
            out[base + 3 : base + 5] = kn[faces] * shut
            if lo:
                out[base + 2 : base + 3] = un[7:8] * ocean[7:8]
                out[base + 5 : base + 6] = kn[7:8] * ocean[7:8]
            open_e = ocean * beside
            out[base + 6 : base + 8] = (ue_ref[lev, tile] * (1.0 / 12.0) * open_e)[rows]
            out[base + 8 : base + 10] = (ke_ref[lev, tile] * open_e)[rows]
            out[base + 10 : base + 12] = ocean[rows]
            for t in range(2):
                q = t_ref[t, lev, tile] * ocean
                m = 3 * t + lev
                out[4 * m : 4 * m + 4] = q[4:8] if lo else q[0:4]
    even = lax.rem(lax.axis_index("lat"), 2) == 0
    north, south = nb[...], sb[...]
    a_ref[...] = jnp.where(even, north, south)
    b_ref[...] = jnp.where(even, south, north)

    def body(i, carry):
        to_e = jnp.zeros((8, 128), F32)
        to_w = jnp.zeros((8, 128), F32)
        for g in range(GROUPS):
            blk = rows_of(i, g)
            for lev in range(LEV):
                ocean = m_ref[lev, blk].astype(F32)
                u = ue_ref[lev, blk] * (1.0 / 12.0) * ocean
                k = ke_ref[lev, blk] * ocean
                at = 32 * g + 24 + lev
                to_e = place(to_e, u, 127, at, 1, lane)
                to_e = place(to_e, k, 127, at + 3, 1, lane)
                to_w = place(to_w, ocean, 0, at, 1, lane)
                for t in range(2):
                    q = t_ref[t, lev, blk] * ocean
                    at = 32 * g + 4 * (3 * t + lev)
                    to_e = place(to_e, q, 126, at, 2, lane)
                    to_w = place(to_w, q, 0, at + 2, 2, lane)
        out = pl.ds(pl.multiple_of(i * 8, 8), 8)
        e_ref[out] = to_e
        w_ref[out] = to_w
        return carry

    lax.fori_loop(0, BLOCKS, body, 0)


def flip(x):
    lane = lax.broadcasted_iota(jnp.int32, x.shape, 1)
    for s in (1, 2, 4, 8, 16, 32, 64):
        x = jnp.where((lane & s) != 0, roll(x, s), roll(x, -s))
    return x


def step_kernel(
    t_ref, ue_ref, un_ref, ke_ref, kn_ref, m_ref, re_ref, rw_ref, ra_ref, rb_ref,
    wt_ref, q1_ref, hc_ref, hq_ref, e_ref, w_ref,
    q0, os, nu, nk, nh, sh,
):
    lane = lanes()
    lat = lax.axis_index("lat")
    even = lax.rem(lat, 2) == 0
    southern = lat == 0
    northern = lat == lax.axis_size("lat") - 1
    first, second = ra_ref[...], rb_ref[...]
    sh[...] = jnp.where(southern, 0.0, jnp.where(even, second, first))
    nh[...] = jnp.where(even, first, second)

    @pl.when(northern)
    def _():
        f = flip(rb_ref[...])
        shifted = roll(f, -1)
        for m in range(MEM):
            for r in range(4):
                nh[4 * m + r : 4 * m + r + 1] = f[4 * m + 3 - r : 4 * m + 4 - r]
        for lev in range(LEV):
            base = 24 + 12 * lev
            for to, source, x in (
                (0, 1, -f), (1, 0, -f), (2, 2, -f), (3, 4, f), (4, 3, f), (5, 5, f),
                (6, 7, -shifted), (7, 6, -shifted), (8, 9, shifted), (9, 8, shifted), (10, 11, f), (11, 10, f),
            ):
                nh[base + to : base + to + 1] = x[base + source : base + source + 1]

    for m in range(MEM):
        q0[m, 4:8] = sh[4 * m : 4 * m + 4]
        q0[m, 264:268] = nh[4 * m : 4 * m + 4]

    def fill(i, carry):
        blk = pl.ds(pl.multiple_of(i * 8, 8), 8)
        own = pl.ds(pl.multiple_of(i * 8, 8) + 8, 8)
        for lev in range(LEV):
            ocean = m_ref[lev, blk].astype(F32)
            os[lev, own] = ocean
            for t in range(2):
                q0[3 * t + lev, own] = t_ref[t, lev, blk] * ocean
        return carry

    lax.fori_loop(0, ROWS // 8, fill, 0)
    for lev in range(LEV):
        base = 24 + 12 * lev
        top = os[lev, 263:264]
        os[lev, 264:265] = jnp.where(northern, top, nh[base + 10 : base + 11])
        low = os[lev, 8:9]
        nu[lev, 7:8] = sh[base + 2 : base + 3] * low
        nk[lev, 7:8] = sh[base + 5 : base + 6] * low

    def faces(i, carry):
        at = pl.multiple_of(i * 8, 8)
        blk, own, above = pl.ds(at, 8), pl.ds(at + 8, 8), pl.ds(at + 9, 8)
        for lev in range(LEV):
            shut = os[lev, own] * os[lev, above]
            nu[lev, own] = un_ref[lev, blk] * (1.0 / 12.0) * shut
            nk[lev, own] = kn_ref[lev, blk] * shut
        return carry

    lax.fori_loop(0, ROWS // 8, faces, 0)

    def body(i, carry):
        at = pl.multiple_of(i * 8, 8)
        out = pl.ds(at, 8)
        from_w, from_e = re_ref[out], rw_ref[out]
        both = jnp.where((lane & 2) == 0, from_w, from_e)
        to_e = jnp.zeros((8, 128), F32)
        to_w = jnp.zeros((8, 128), F32)
        for g in range(GROUPS):
            blk = rows_of(i, g)

            def near(k, at=at, g=g):
                return pl.ds(at + (64 * g + 8 + k), 8)

            for lev in range(LEV):
                ocean = os[lev, near(0)]
                spot = 32 * g + 24 + lev
                beside = jnp.where(lane == 127, roll(from_e, 127 - spot), roll(ocean, -1))
                shut = ocean * beside
                u = ue_ref[lev, blk] * (1.0 / 12.0) * shut
                k = ke_ref[lev, blk] * shut
                uw = jnp.where(lane == 0, roll(from_w, -spot) * ocean, roll(u, 1))
                kw = jnp.where(lane == 0, roll(from_w, -(spot + 3)) * ocean, roll(k, 1))
                north = nu[lev, near(0)], nk[lev, near(0)]
                south = nu[lev, near(-1)], nk[lev, near(-1)]
                w = weigh(ocean, (u, k), (uw, kw), north, south)
                for n in range(9):
                    wt_ref[9 * lev + n, blk] = w[n]
                for t in range(2):
                    m = 3 * t + lev
                    spot = 32 * g + 4 * m
                    sides = roll(both, 126 - spot)
                    new = apply(
                        w, q0[m, near(0)], sides, q0[m, near(-2)], q0[m, near(-1)], q0[m, near(1)], q0[m, near(2)], lane
                    )
                    q1_ref[m, blk] = new
                    to_e = place(to_e, new, 126, spot, 2, lane)
                    to_w = place(to_w, new, 0, spot + 2, 2, lane)
        e_ref[out] = to_e
        w_ref[out] = to_w
        return carry

    lax.fori_loop(0, BLOCKS, body, 0)

    hc_ref[...] = jnp.zeros((7 * LEV, 8, 128), F32)
    hq_ref[...] = jnp.zeros((5 * MEM, 8, 128), F32)
    for lev in range(LEV):
        base = 24 + 12 * lev
        for n, (ref, slot) in enumerate(((nu, 0), (nk, 3))):
            lower = jnp.where(northern, nh[base + slot + 2 : base + slot + 3], ref[lev, 263:264])
            hc_ref[7 * lev + n, 0:2] = sh[base + slot : base + slot + 2]
            hc_ref[7 * lev + n, 2:3] = lower
            hc_ref[7 * lev + n, 3:4] = nh[base + slot : base + slot + 1]
            hc_ref[7 * lev + 2 + n, 0:1] = sh[base + slot + 1 : base + slot + 2]
            hc_ref[7 * lev + 2 + n, 1:2] = ref[lev, 7:8]
            hc_ref[7 * lev + 2 + n, 2:4] = nh[base + slot : base + slot + 2]
        for n in range(3):
            hc_ref[7 * lev + 4 + n, 0:2] = sh[base + 6 + 2 * n : base + 8 + 2 * n]
            hc_ref[7 * lev + 4 + n, 2:4] = nh[base + 6 + 2 * n : base + 8 + 2 * n]
    for m in range(MEM):
        for k in range(5):
            hq_ref[6 * k + m, 0:2] = q0[m, 4 + k : 6 + k]
            hq_ref[6 * k + m, 2:4] = q0[m, 262 + k : 264 + k]
    to_e = jnp.zeros((8, 128), F32)
    to_w = jnp.zeros((8, 128), F32)
    for m in range(MEM):
        q = hq_ref[12 + m]
        to_e = place(to_e, q, 126, 4 * m, 2, lane)
        to_w = place(to_w, q, 0, 4 * m + 2, 2, lane)
    for lev in range(LEV):
        u, k, ocean = hc_ref[7 * lev + 4], hc_ref[7 * lev + 5], hc_ref[7 * lev + 6]
        for x, spot in ((u, 32), (k, 35), (ocean, 38)):
            to_e = place(to_e, x, 127, spot + lev, 1, lane)
            to_w = place(to_w, x, 0 if spot == 38 else 127, spot + lev, 1, lane)
    e_ref[64:72] = to_e
    w_ref[64:72] = to_w


def last_kernel(wt_ref, q1_ref, hc_ref, hq_ref, re_ref, rw_ref, out_ref, qs):
    lane = lanes()
    row = lax.broadcasted_iota(jnp.int32, (8, 128), 0)
    northern = lax.axis_index("lat") == lax.axis_size("lat") - 1
    folded = (row >= 2) & northern

    def fill(i, carry):
        blk = pl.ds(pl.multiple_of(i * 8, 8), 8)
        own = pl.ds(pl.multiple_of(i * 8, 8) + 8, 8)
        for m in range(MEM):
            qs[m, own] = q1_ref[m, blk]
        return carry

    lax.fori_loop(0, ROWS // 8, fill, 0)
    from_w, from_e = re_ref[64:72], rw_ref[64:72]
    both = jnp.where((lane & 2) == 0, from_w, from_e)
    for lev in range(LEV):
        ulo, klo, uup, kup, u, k, ocean = (hc_ref[7 * lev + n] for n in range(7))
        ocean_w = roll(from_w, -(38 + lev))
        ocean_e = roll(from_e, 127 - 38 - lev)

        def ends(x, spot, ocean=ocean, ocean_w=ocean_w, ocean_e=ocean_e):
            east = jnp.where(folded, roll(from_e, 127 - spot) * ocean, x * ocean_e)
            west = jnp.where(folded, roll(x, 1) * ocean_w, roll(from_w, -spot) * ocean)
            return jnp.where(lane == 127, east, x), jnp.where(lane == 0, west, roll(x, 1))

        ue, uw = ends(u, 32 + lev)
        ke, kw = ends(k, 35 + lev)
        w = weigh(ocean, (ue, ke), (uw, kw), (uup, kup), (ulo, klo))
        for t in range(2):
            m = 3 * t + lev
            q = [hq_ref[6 * n + m] for n in range(5)]
            new = apply(w, q[2], roll(both, 126 - 4 * m), q[0], q[1], q[3], q[4], lane)
            qs[m, 6:8] = new[0:2]
            qs[m, 264:266] = new[2:4]

    def body(i, carry):
        at = pl.multiple_of(i * 8, 8)
        both = jnp.where((lane & 2) == 0, re_ref[pl.ds(at, 8)], rw_ref[pl.ds(at, 8)])
        for g in range(GROUPS):
            blk = rows_of(i, g)

            def near(k, at=at, g=g):
                return pl.ds(at + (64 * g + 8 + k), 8)

            for lev in range(LEV):
                w = [wt_ref[9 * lev + n, blk] for n in range(9)]
                for t in range(2):
                    m = 3 * t + lev
                    sides = roll(both, 126 - 32 * g - 4 * m)
                    out_ref[t, lev, blk] = apply(
                        w, qs[m, near(0)], sides, qs[m, near(-2)], qs[m, near(-1)], qs[m, near(1)], qs[m, near(2)], lane
                    )
        return carry

    lax.fori_loop(0, BLOCKS, body, 0)


def call(kernel, shapes, scratch, name, *operands):
    vmem = pl.BlockSpec(memory_space=pltpu.VMEM)
    return pl.pallas_call(
        kernel,
        out_shape=[jax.ShapeDtypeStruct(s, F32) for s in shapes],
        in_specs=[vmem] * len(operands),
        out_specs=[vmem] * len(shapes),
        scratch_shapes=[pltpu.VMEM(s, F32) for s in scratch],
        compiler_params=pltpu.CompilerParams(vmem_limit_bytes=16 * 2**20),
        name=name,
    )(*operands)


def patterns(height, width):
    def flat(make):
        return [
            (lat * width + lon, (to[0] % height) * width + to[1] % width)
            for lat in range(height)
            for lon in range(width)
            for to in [make(lat, lon)]
        ]

    def odd(pivot):
        def make(lat, lon):
            if lat == height - 1:
                return lat, pivot - 1 - lon
            if lat == 0:
                return lat, lon
            return (lat + 1, lon) if lat % 2 else (lat - 1, lon)

        return flat(make)

    east = flat(lambda lat, lon: (lat, lon + 1))
    west = flat(lambda lat, lon: (lat, lon - 1))
    pairs = flat(lambda lat, lon: (lat + 1, lon) if lat % 2 == 0 else (lat - 1, lon))
    return east, west, pairs, odd


def local(height, width, tracers, east_courant, north_courant, east_kappa, north_kappa, ocean_mask, fold_map):
    east, west, pairs, odd = patterns(height, width)
    fields = (tracers, east_courant, north_courant, east_kappa, north_kappa, ocean_mask)
    pivot = ((fold_map[0] + 1) // 128 + lax.axis_index("lon")) % width
    edge = (64, 128)
    a, b, e, w = call(pack_kernel, [edge] * 4, [edge] * 2, "pack", *fields)
    re = lax.ppermute(e, BOTH, east)
    rw = lax.ppermute(w, BOTH, west)
    ra = lax.ppermute(a, BOTH, pairs)
    rb = lax.switch(pivot, [lambda x, p=p: lax.ppermute(x, BOTH, odd(p)) for p in range(width)], b)
    ext = (LEV, ROWS + 16, 128)
    wt, q1, hc, hq, e, w = call(
        step_kernel,
        [(9 * LEV, ROWS, 128), (MEM, ROWS, 128), (7 * LEV, 8, 128), (5 * MEM, 8, 128), (72, 128), (72, 128)],
        [(MEM, ROWS + 16, 128), ext, ext, ext, edge, edge],
        "step",
        *fields, re, rw, ra, rb,
    )
    re = lax.ppermute(e, BOTH, east)
    rw = lax.ppermute(w, BOTH, west)
    [out] = call(last_kernel, [(2, LEV, ROWS, 128)], [(MEM, ROWS + 16, 128)], "last", wt, q1, hc, hq, re, rw)
    return out


def solution(mesh):
    plane = P(None, "lat", "lon")
    grid = P(None, None, "lat", "lon")
    return jax.shard_map(
        functools.partial(local, mesh.shape["lat"], mesh.shape["lon"]),
        mesh=mesh,
        in_specs=(grid, plane, plane, plane, plane, plane, P("lon")),
        out_specs=grid,
        check_vma=False,
    )
```

time: 183 us -> 47.5 us (0.26)
  blocking collectives: 69.2 us -> 0 us
  local copies, waits for them, and re-layouts: 58.5 us -> 12.2 us
  other arithmetic: 23.2 us -> 0 us
  starting transfers between devices: 30 us -> 15.9 us
  Pallas kernels: 0 us -> 11.1 us
  waiting for transfers between devices: 0.03 us -> 6.84 us
    all_gather x2 -> x0, blocking collectives: 69.2 us -> none  [local(): piece = lax.all_gather(top, 'lon', axis=3, tiled=True)]
    slice x29 -> x0, local copies, waits for them, and re-layouts: 21.4 us -> none  [the longest x5 5.7 us: extended(): lax.slice_in_dim(cells, cells.shape[dim] - width, cells.shape[dim], axis=...]
    mul x12 -> x0, other arithmetic: 17.3 us -> none  [the longest x6 11.7 us: face_flux(): opened * (courant * centered / 12.0 - jnp.abs(courant) * upwind / 12.0 -...]
    all_gather x2 -> x0, local copies, waits for them, and re-layouts: 16.1 us -> none  [local(): piece = lax.all_gather(top, 'lon', axis=3, tiled=True)]
    ppermute x12 -> x6, starting transfers between devices: 30 us -> 15.9 us  [the longest x2 9.85 us: local(): rw = lax.ppermute(w, BOTH, west)]
    pallas_call x0 -> x3, Pallas kernels: none -> 11.1 us  [call(): pl.pallas_call(kernel, out_shape=[jax.ShapeDtypeStruct(s, F32) for s in s...]
    gather x4 -> x0, local copies, waits for them, and re-layouts: 9.15 us -> none  [local(): picked = jnp.take(piece, jnp.clip(fold_map, 0, piece.shape[3] - 1), axis=3)]
    ppermute x12 -> x6, waiting for transfers between devices: 0.03 us -> 6.84 us  [the longest x1 5.19 us: local(): lax.ppermute(x, BOTH, odd(p))]
  transfers between devices with their start and end apart: 12 -> 6, of which waited for: 0 -> 2; matrix products, arithmetic and copies ran while one was open for 31% -> 0% of each run, Pallas kernels for 0% -> 0%
where the time goes in v1:
time: 47.5 us; the launch traced here: 46.8 us
  starting transfers between devices  15.9 us (33%)
  local copies, waits for them, and re-layouts  12.2 us (26%)
  Pallas kernels  11.1 us (23%)
  waiting for transfers between devices  6.84 us (14%)
  between operations  0.75 us (2%)
    unnamed x24, local copies, waits for them, and re-layouts  12.2 us
    pallas_call x3, Pallas kernels, call(): pl.pallas_call(kernel, out_shape=[jax.ShapeDtypeStruct(s, F32) for s in s...  11.1 us
    ppermute x2, starting transfers between devices, local(): rw = lax.ppermute(w, BOTH, west)  9.85 us
    ppermute x1, waiting for transfers between devices, local(): lax.ppermute(x, BOTH, odd(p))  5.19 us
    ppermute x1, starting transfers between devices, local(): lax.ppermute(x, BOTH, odd(p))  4.33 us
    ppermute x2, waiting for transfers between devices, local(): re = lax.ppermute(e, BOTH, east)  1.64 us
    ppermute x1, starting transfers between devices, local(): ra = lax.ppermute(a, BOTH, pairs)  1.58 us
  transfers between devices with their start and end apart: 6, of which 2 were waited for; matrix products, arithmetic and copies ran while one was open for 0% of the time, Pallas kernels for 0%

profile of v1, /device:TPU:4, one launch (start us, length us, event | category | flops | bytes accessed | tf_op | source)
XLA Modules:
  0.0 46.8 jit_solution(12674827054479639576)
XLA Ops:
  0.0 1.1 %copy-done = f32[2,3,256,128]{3,2,1,0:T(8,128)S(1)} copy-done((f32[2,3,256,128]{3,2,1,0:T(8,128)S(1)}, f32[2,3,256,128]{3,2,1,0:T(8,128)}, u32[]{:S(2)}) %copy-start) | copy-done | bytes 786456
  1.1 1.0 %copy-done.2 = f32[3,256,128]{2,1,0:T(8,128)S(1)} copy-done((f32[3,256,128]{2,1,0:T(8,128)S(1)}, f32[3,256,128]{2,1,0:T(8,128)}, u32[]{:S(2)}) %copy-start.2) | copy-done | bytes 393240
  2.1 1.0 %copy-done.4 = f32[3,256,128]{2,1,0:T(8,128)S(1)} copy-done((f32[3,256,128]{2,1,0:T(8,128)S(1)}, f32[3,256,128]{2,1,0:T(8,128)}, u32[]{:S(2)}) %copy-start.4) | copy-done | bytes 393240
  3.1 1.0 %copy-done.6 = f32[3,256,128]{2,1,0:T(8,128)S(1)} copy-done((f32[3,256,128]{2,1,0:T(8,128)S(1)}, f32[3,256,128]{2,1,0:T(8,128)}, u32[]{:S(2)}) %copy-start.6) | copy-done | bytes 393240
  4.1 1.0 %copy-done.8 = f32[3,256,128]{2,1,0:T(8,128)S(1)} copy-done((f32[3,256,128]{2,1,0:T(8,128)S(1)}, f32[3,256,128]{2,1,0:T(8,128)}, u32[]{:S(2)}) %copy-start.8) | copy-done | bytes 393240
  5.1 1.0 %copy-done.10 = s32[3,256,128]{2,1,0:T(8,128)S(1)} copy-done((s32[3,256,128]{2,1,0:T(8,128)S(1)}, s32[3,256,128]{2,1,0:T(8,128)}, u32[]{:S(2)}) %copy-start.10) | copy-done | bytes 393240
  6.1 1.2 %pack.1 = (f32[64,128]{1,0:T(8,128)S(1)}, f32[64,128]{1,0:T(8,128)S(1)}, f32[64,128]{1,0:T(8,128)S(1)}, f32[64,128]{1,0:T(8,128)S(1)}) custom-call(f32[2,3,256,128]{3,2,1,0:T(8,128)S(1)} %copy-done, f32[3,256,128]{2,1,0:T(8,128)S(1)} %copy-done.2, f32[3,256,128]{2,1,0:T(8,128)S(1)} %copy-done.4, f32[3,256,128]{2,1,0:T(8,128)S(1)} %copy-done.6, ...), custom_call_target="tpu_custom_call" | custom-call | tf_op jit(solution)/shard_map/pack/pallas_call | solution.py:341
  7.3 0.1 collective-permute-start.32
  7.4 6.0 %collective-permute-start.33 = (f32[64,128]{1,0:T(8,128)S(1)}, f32[64,128]{1,0:T(8,128)S(1)}, u32[]{:S(2)}, u32[]{:S(2)}) collective-permute-start(f32[64,128]{1,0:T(8,128)S(1)} %get-tuple-element.81), channel_id=1, source_target_pairs={{0,31},{1,0},{2,1},{3,2},{4,3},{5,4},{6,5},{7,6},{8,7},{9,8},{10,9... | collective-permute-start | bytes 98312 | tf_op jit(solution)/shard_map/ppermute | solution.py:384
  13.4 1.6 %collective-permute-start.34 = (f32[64,128]{1,0:T(8,128)S(1)}, f32[64,128]{1,0:T(8,128)S(1)}, u32[]{:S(2)}, u32[]{:S(2)}) collective-permute-start(f32[64,128]{1,0:T(8,128)S(1)} %get-tuple-element.82), channel_id=1, source_target_pairs={{0,32},{1,33},{2,34},{3,35},{4,36},{5,37},{6,38},{7,39},{8,40},{9,... | collective-permute-start | bytes 98312 | tf_op jit(solution)/shard_map/ppermute | solution.py:385
  15.7 9.6 %conditional.1 = (f32[64,128]{1,0:T(8,128)}) conditional(s32[]{:T(128)} %clamp.3, f32[64,128]{1,0:T(8,128)S(1)} %get-tuple-element.83, f32[64,128]{1,0:T(8,128)S(1)} %get-tuple-element.83, f32[64,128]{1,0:T(8,128)S(1)} %get-tuple-element.83, f32[64,128]{1,0:T(8,128)S(1)} %get-tuple-element.83, ...), branch_computations={%region_0.1_spmd, %region_1.2_spmd, %region_2.3_spmd, %region_3.4_... | conditional | bytes 131120 | solution.py:386
  15.7 4.3 %collective-permute-start.5 = (f32[64,128]{1,0:T(8,128)S(1)}, f32[64,128]{1,0:T(8,128)}, u32[]{:S(2)}, u32[]{:S(2)}) collective-permute-start(f32[64,128]{1,0:T(8,128)S(1)} %param.5), channel_id=1, source_target_pairs={{0,0},{1,1},{2,2},{3,3},{4,4},{5,5},{6,6},{7,7},{8,8},{9,9},{10,10... | collective-permute-start | bytes 98312 | tf_op jit(solution)/shard_map/cond/branch_5_fun/ppermute | solution.py:386
  20.1 5.2 %collective-permute-done.5 = f32[64,128]{1,0:T(8,128)} collective-permute-done((f32[64,128]{1,0:T(8,128)S(1)}, f32[64,128]{1,0:T(8,128)}, u32[]{:S(2)}, u32[]{:S(2)}) %collective-permute-start.5) | collective-permute-done | bytes 32800 | tf_op jit(solution)/shard_map/cond/branch_5_fun/ppermute | solution.py:386
  25.3 1.1 %copy-done.1 = f32[2,3,256,128]{3,2,1,0:T(8,128)S(1)} copy-done((f32[2,3,256,128]{3,2,1,0:T(8,128)S(1)}, f32[2,3,256,128]{3,2,1,0:T(8,128)}, u32[]{:S(2)}) %copy-start.1) | copy-done | bytes 786456
  26.4 1.0 %copy-done.3 = f32[3,256,128]{2,1,0:T(8,128)S(1)} copy-done((f32[3,256,128]{2,1,0:T(8,128)S(1)}, f32[3,256,128]{2,1,0:T(8,128)}, u32[]{:S(2)}) %copy-start.3) | copy-done | bytes 393240
  27.4 1.0 %copy-done.5 = f32[3,256,128]{2,1,0:T(8,128)S(1)} copy-done((f32[3,256,128]{2,1,0:T(8,128)S(1)}, f32[3,256,128]{2,1,0:T(8,128)}, u32[]{:S(2)}) %copy-start.5) | copy-done | bytes 393240
  28.4 1.0 %copy-done.7 = f32[3,256,128]{2,1,0:T(8,128)S(1)} copy-done((f32[3,256,128]{2,1,0:T(8,128)S(1)}, f32[3,256,128]{2,1,0:T(8,128)}, u32[]{:S(2)}) %copy-start.7) | copy-done | bytes 393240
  29.4 1.0 %copy-done.9 = f32[3,256,128]{2,1,0:T(8,128)S(1)} copy-done((f32[3,256,128]{2,1,0:T(8,128)S(1)}, f32[3,256,128]{2,1,0:T(8,128)}, u32[]{:S(2)}) %copy-start.9) | copy-done | bytes 393240
  30.4 1.0 %copy-done.11 = s32[3,256,128]{2,1,0:T(8,128)S(1)} copy-done((s32[3,256,128]{2,1,0:T(8,128)S(1)}, s32[3,256,128]{2,1,0:T(8,128)}, u32[]{:S(2)}) %copy-start.11) | copy-done | bytes 393240
  31.4 6.6 %step.1 = (f32[27,256,128]{2,1,0:T(8,128)S(1)}, f32[6,256,128]{2,1,0:T(8,128)S(1)}, f32[21,8,128]{2,1,0:T(8,128)S(1)}, f32[30,8,128]{2,1,0:T(8,128)S(1)}, f32[72,128]{1,0:T(8,128)S(1)}, /*index=5*/f32[72,128]{1,0:T(8,128)S(1)}) custom-call(f32[2,3,256,128]{3,2,1,0:T(8,128)S(1)} %copy-done.1, f32[3,256,128]{2,1,0:T(8,128)S(1)} %copy-done.3, ...), custom_call_target="tpu_custom_call" | custom-call | tf_op jit(solution)/shard_map/step/pallas_call | solution.py:341
  38.0 0.1 collective-permute-start.35
  38.1 3.8 %collective-permute-start.36 = (f32[72,128]{1,0:T(8,128)S(1)}, f32[72,128]{1,0:T(8,128)S(1)}, u32[]{:S(2)}, u32[]{:S(2)}) collective-permute-start(f32[72,128]{1,0:T(8,128)S(1)} %get-tuple-element.89), channel_id=1, source_target_pairs={{0,31},{1,0},{2,1},{3,2},{4,3},{5,4},{6,5},{7,6},{8,7},{9,8},{10,9... | collective-permute-start | bytes 110600 | tf_op jit(solution)/shard_map/ppermute | solution.py:396
  41.9 1.6 %collective-permute-done.35.re_ref = f32[72,128]{1,0:T(8,128)S(1)} collective-permute-done((f32[72,128]{1,0:T(8,128)S(1)}, f32[72,128]{1,0:T(8,128)S(1)}, u32[]{:S(2)}, u32[]{:S(2)}) %collective-permute-start.35) | collective-permute-done | bytes 36896 | tf_op jit(solution)/shard_map/ppermute | solution.py:395
  43.5 3.3 %last.1 = f32[2,3,256,128]{3,2,1,0:T(8,128)} custom-call(f32[27,256,128]{2,1,0:T(8,128)S(1)} %get-tuple-element.84.wt_ref, f32[6,256,128]{2,1,0:T(8,128)S(1)} %get-tuple-element.85.q1_ref, f32[21,8,128]{2,1,0:T(8,128)S(1)} %get-tuple-element.86.hc_ref, f32[30,8,128]{2,1,0:T(8,128)S(1)} %get-tuple-element.87.hq_ref, ...), custom_call_target="tpu_custom_call" | custom-call | tf_op jit(solution)/shard_map/last/pallas_call | solution.py:341
  (16 shorter events, 0.0 us)
Async XLA Ops:
  0.0 1.1 %copy-start = (f32[2,3,256,128]{3,2,1,0:T(8,128)S(1)}, f32[2,3,256,128]{3,2,1,0:T(8,128)}, u32[]{:S(2)}) copy-start(f32[2,3,256,128]{3,2,1,0:T(8,128)} %t_ref.3) | copy-start | bytes 2359300
  1.1 1.0 %copy-start.2 = (f32[3,256,128]{2,1,0:T(8,128)S(1)}, f32[3,256,128]{2,1,0:T(8,128)}, u32[]{:S(2)}) copy-start(f32[3,256,128]{2,1,0:T(8,128)} %ue_ref.3) | copy-start | bytes 1179652
  2.1 1.0 %copy-start.4 = (f32[3,256,128]{2,1,0:T(8,128)S(1)}, f32[3,256,128]{2,1,0:T(8,128)}, u32[]{:S(2)}) copy-start(f32[3,256,128]{2,1,0:T(8,128)} %un_ref.3) | copy-start | bytes 1179652
  3.1 1.0 %copy-start.6 = (f32[3,256,128]{2,1,0:T(8,128)S(1)}, f32[3,256,128]{2,1,0:T(8,128)}, u32[]{:S(2)}) copy-start(f32[3,256,128]{2,1,0:T(8,128)} %ke_ref.3) | copy-start | bytes 1179652
  4.1 1.0 %copy-start.8 = (f32[3,256,128]{2,1,0:T(8,128)S(1)}, f32[3,256,128]{2,1,0:T(8,128)}, u32[]{:S(2)}) copy-start(f32[3,256,128]{2,1,0:T(8,128)} %kn_ref.3) | copy-start | bytes 1179652
  5.1 1.0 %copy-start.10 = (s32[3,256,128]{2,1,0:T(8,128)S(1)}, s32[3,256,128]{2,1,0:T(8,128)}, u32[]{:S(2)}) copy-start(s32[3,256,128]{2,1,0:T(8,128)} %m_ref.3) | copy-start | bytes 1179652
  7.3 17.9 %collective-permute-start.32 = (f32[64,128]{1,0:T(8,128)S(1)}, f32[64,128]{1,0:T(8,128)S(1)}, u32[]{:S(2)}, u32[]{:S(2)}) collective-permute-start(f32[64,128]{1,0:T(8,128)S(1)} %get-tuple-element.80), channel_id=1, source_target_pairs={{0,1},{1,2},{2,3},{3,4},{4,5},{5,6},{6,7},{7,8},{8,9},{9,10},{10,1... | collective-permute-start | bytes 98312 | tf_op jit(solution)/shard_map/ppermute | solution.py:383
  7.4 17.8 %collective-permute-start.33 = (f32[64,128]{1,0:T(8,128)S(1)}, f32[64,128]{1,0:T(8,128)S(1)}, u32[]{:S(2)}, u32[]{:S(2)}) collective-permute-start(f32[64,128]{1,0:T(8,128)S(1)} %get-tuple-element.81), channel_id=1, source_target_pairs={{0,31},{1,0},{2,1},{3,2},{4,3},{5,4},{6,5},{7,6},{8,7},{9,8},{10,9... | collective-permute-start | bytes 98312 | tf_op jit(solution)/shard_map/ppermute | solution.py:384
  13.4 11.8 %collective-permute-start.34 = (f32[64,128]{1,0:T(8,128)S(1)}, f32[64,128]{1,0:T(8,128)S(1)}, u32[]{:S(2)}, u32[]{:S(2)}) collective-permute-start(f32[64,128]{1,0:T(8,128)S(1)} %get-tuple-element.82), channel_id=1, source_target_pairs={{0,32},{1,33},{2,34},{3,35},{4,36},{5,37},{6,38},{7,39},{8,40},{9,... | collective-permute-start | bytes 98312 | tf_op jit(solution)/shard_map/ppermute | solution.py:385
  15.7 9.5 %collective-permute-start.5 = (f32[64,128]{1,0:T(8,128)S(1)}, f32[64,128]{1,0:T(8,128)}, u32[]{:S(2)}, u32[]{:S(2)}) collective-permute-start(f32[64,128]{1,0:T(8,128)S(1)} %param.5), channel_id=1, source_target_pairs={{0,0},{1,1},{2,2},{3,3},{4,4},{5,5},{6,6},{7,7},{8,8},{9,9},{10,10... | collective-permute-start | bytes 98312 | tf_op jit(solution)/shard_map/cond/branch_5_fun/ppermute | solution.py:386
  25.3 1.1 %copy-start.1 = (f32[2,3,256,128]{3,2,1,0:T(8,128)S(1)}, f32[2,3,256,128]{3,2,1,0:T(8,128)}, u32[]{:S(2)}) copy-start(f32[2,3,256,128]{3,2,1,0:T(8,128)} %t_ref.3) | copy-start | bytes 2359300
  26.4 1.0 %copy-start.3 = (f32[3,256,128]{2,1,0:T(8,128)S(1)}, f32[3,256,128]{2,1,0:T(8,128)}, u32[]{:S(2)}) copy-start(f32[3,256,128]{2,1,0:T(8,128)} %ue_ref.3) | copy-start | bytes 1179652
  27.4 1.0 %copy-start.5 = (f32[3,256,128]{2,1,0:T(8,128)S(1)}, f32[3,256,128]{2,1,0:T(8,128)}, u32[]{:S(2)}) copy-start(f32[3,256,128]{2,1,0:T(8,128)} %un_ref.3) | copy-start | bytes 1179652
  28.4 1.0 %copy-start.7 = (f32[3,256,128]{2,1,0:T(8,128)S(1)}, f32[3,256,128]{2,1,0:T(8,128)}, u32[]{:S(2)}) copy-start(f32[3,256,128]{2,1,0:T(8,128)} %ke_ref.3) | copy-start | bytes 1179652
  29.4 1.0 %copy-start.9 = (f32[3,256,128]{2,1,0:T(8,128)S(1)}, f32[3,256,128]{2,1,0:T(8,128)}, u32[]{:S(2)}) copy-start(f32[3,256,128]{2,1,0:T(8,128)} %kn_ref.3) | copy-start | bytes 1179652
  30.4 1.0 %copy-start.11 = (s32[3,256,128]{2,1,0:T(8,128)S(1)}, s32[3,256,128]{2,1,0:T(8,128)}, u32[]{:S(2)}) copy-start(s32[3,256,128]{2,1,0:T(8,128)} %m_ref.3) | copy-start | bytes 1179652
  38.0 5.6 %collective-permute-start.35 = (f32[72,128]{1,0:T(8,128)S(1)}, f32[72,128]{1,0:T(8,128)S(1)}, u32[]{:S(2)}, u32[]{:S(2)}) collective-permute-start(f32[72,128]{1,0:T(8,128)S(1)} %get-tuple-element.88), channel_id=1, source_target_pairs={{0,1},{1,2},{2,3},{3,4},{4,5},{5,6},{6,7},{7,8},{8,9},{9,10},{10,1... | collective-permute-start | bytes 110600 | tf_op jit(solution)/shard_map/ppermute | solution.py:395
  38.1 5.5 %collective-permute-start.36 = (f32[72,128]{1,0:T(8,128)S(1)}, f32[72,128]{1,0:T(8,128)S(1)}, u32[]{:S(2)}, u32[]{:S(2)}) collective-permute-start(f32[72,128]{1,0:T(8,128)S(1)} %get-tuple-element.89), channel_id=1, source_target_pairs={{0,31},{1,0},{2,1},{3,2},{4,3},{5,4},{6,5},{7,6},{8,7},{9,8},{10,9... | collective-permute-start | bytes 110600 | tf_op jit(solution)/shard_map/ppermute | solution.py:396

commit v2 on v1

v2 whole, which is shorter than its diff:
```python
import functools

import jax
import jax.numpy as jnp
from jax import lax
from jax.experimental import pallas as pl
from jax.experimental.pallas import tpu as pltpu
from jax.sharding import PartitionSpec as P

BOTH = ("lat", "lon")
LEV = 3
MEM = 6
ROWS = 256
BLOCKS = 8
GROUPS = 4
TWELFTH = 1.0 / 12.0
F32 = jnp.float32


def lanes():
    return lax.broadcasted_iota(jnp.int32, (8, 128), 1)


def roll(x, shift):
    shift = shift % 128
    return x if shift == 0 else pltpu.roll(x, shift, axis=1)


def face(courant, kappa):
    size = jnp.abs(courant)
    slope = 3.0 * size + kappa
    seven = 7.0 * courant
    return -(courant + size), seven + slope, seven - slope, size - courant


def weigh(ocean, east, west, north, south):
    ea, eb, ec, ed = face(*east)
    wa, wb, wc, wd = face(*west)
    na, nb, nc, nd = face(*north)
    sa, sb, sc, sd = face(*south)
    return (
        ocean + ((wc - eb) + (sc - nb)),
        wa,
        wb - ea,
        wd - ec,
        -ed,
        sa,
        sb - na,
        sd - nc,
        -nd,
    )


def apply(w, q, sides, below2, below1, above1, above2, lane):
    west2 = roll(jnp.where(lane >= 126, sides, q), 2)
    west1 = roll(jnp.where(lane == 127, sides, q), 1)
    east1 = roll(jnp.where(lane == 0, sides, q), -1)
    east2 = roll(jnp.where(lane < 2, sides, q), -2)
    across = (w[1] * west2 + w[2] * west1) + (w[3] * east1 + w[4] * east2)
    along = (w[5] * below2 + w[6] * below1) + (w[7] * above1 + w[8] * above2)
    return w[0] * q + (across + along)


def place(kept, x, source, target, count, lane):
    moved = roll(x, target - source)
    if count == 1:
        here = lane == target
    else:
        here = (lane >= target) & (lane < target + count)
    return jnp.where(here, moved, kept)


def chunk(i, k=0):
    if isinstance(i, int):
        return pl.ds(32 * i + k, 8)
    return pl.ds(pl.multiple_of(32 * i, 32) + k, 8)


def tile(i):
    return pl.ds(8 * i, 8) if isinstance(i, int) else pl.ds(pl.multiple_of(8 * i, 8), 8)


def pack_kernel(
    t_in, ue_in, un_in, ke_in, kn_in, m_in,
    a_ref, b_ref, e_ref, w_ref, q0, os, un, kn, ue, ke,
    tv, mv, nb, sb, sems,
):
    own = pl.ds(8, ROWS)
    copies = [
        pltpu.make_async_copy(m_in, mv, sems.at[0]),
        pltpu.make_async_copy(t_in, tv, sems.at[1]),
        pltpu.make_async_copy(ue_in, ue, sems.at[2]),
        pltpu.make_async_copy(ke_in, ke, sems.at[3]),
        pltpu.make_async_copy(un_in, un.at[:, own], sems.at[4]),
        pltpu.make_async_copy(kn_in, kn.at[:, own], sems.at[5]),
    ]
    for c in copies:
        c.start()
    lane = lanes()
    nb[...] = jnp.zeros((64, 128), F32)
    sb[...] = jnp.zeros((64, 128), F32)
    for c in copies[:4]:
        c.wait()

    def body(i, carry):
        to_e = jnp.zeros((8, 128), F32)
        to_w = jnp.zeros((8, 128), F32)
        for g in range(GROUPS):
            blk, ext = chunk(i, 8 * g), chunk(i, 8 * g + 8)
            for lev in range(LEV):
                ocean = mv[lev, blk].astype(F32)
                os[lev, ext] = ocean
                at = 32 * g + 24 + lev
                to_e = place(to_e, ue[lev, blk] * ocean, 127, at, 1, lane)
                to_e = place(to_e, ke[lev, blk] * ocean, 127, at + 3, 1, lane)
                to_w = place(to_w, ocean, 0, at, 1, lane)
                for t in range(2):
                    m = 3 * t + lev
                    q = tv[t, lev, blk] * ocean
                    q0[m, ext] = q
                    at = 32 * g + 4 * m
                    to_e = place(to_e, q, 126, at, 2, lane)
                    to_w = place(to_w, q, 0, at + 2, 2, lane)
        e_ref[tile(i)] = to_e
        w_ref[tile(i)] = to_w
        return carry

    lax.fori_loop(0, BLOCKS, body, 0)
    for c in copies[4:]:
        c.wait()
    for lev in range(LEV):
        base = 24 + 12 * lev
        for out, lo, rows, faces in ((nb, ROWS - 8, slice(6, 8), slice(5, 7)), (sb, 0, slice(0, 2), slice(0, 2))):
            blk, ext = pl.ds(lo, 8), pl.ds(lo + 8, 8)
            ocean = os[lev, ext]
            beside = jnp.where(lane == 127, 1.0, roll(ocean, -1))
            up = slice(faces.start + 1, faces.stop + 1)
            shut = ocean[faces] * ocean[up]
            u, k = un[lev, ext], kn[lev, ext]
            out[base : base + 2] = u[faces] * shut
            out[base + 3 : base + 5] = k[faces] * shut
            if lo:
                out[base + 2 : base + 3] = u[7:8] * ocean[7:8]
                out[base + 5 : base + 6] = k[7:8] * ocean[7:8]
            open_e = ocean * beside
            out[base + 6 : base + 8] = (ue[lev, blk] * open_e)[rows]
            out[base + 8 : base + 10] = (ke[lev, blk] * open_e)[rows]
            out[base + 10 : base + 12] = ocean[rows]
            for t in range(2):
                m = 3 * t + lev
                q = q0[m, ext]
                out[4 * m : 4 * m + 4] = q[4:8] if lo else q[0:4]
    even = lax.rem(lax.axis_index("lat"), 2) == 0
    north, south = nb[...], sb[...]
    a_ref[...] = jnp.where(even, north, south)
    b_ref[...] = jnp.where(even, south, north)


def flip(x):
    lane = lax.broadcasted_iota(jnp.int32, x.shape, 1)
    for s in (1, 2, 4, 8, 16, 32, 64):
        x = jnp.where((lane & s) != 0, roll(x, s), roll(x, -s))
    return x


def advance(i, groups, to_e, to_w, lane, q0, os, un, kn, ue, ke, re_ref, rw_ref, wt, q1):
    from_w, from_e = re_ref[tile(i)], rw_ref[tile(i)]
    both = jnp.where((lane & 2) == 0, from_w, from_e)
    for g in groups:
        blk = chunk(i, 8 * g)

        def near(k, g=g):
            return chunk(i, 8 * g + 8 + k)

        for lev in range(LEV):
            ocean = os[lev, near(0)]
            spot = 32 * g + 24 + lev
            beside = jnp.where(lane == 127, roll(from_e, 127 - spot), roll(ocean, -1))
            shut = ocean * beside
            u = ue[lev, blk] * (shut * TWELFTH)
            k = ke[lev, blk] * shut
            uw = jnp.where(lane == 0, roll(from_w, -spot) * (ocean * TWELFTH), roll(u, 1))
            kw = jnp.where(lane == 0, roll(from_w, -(spot + 3)) * ocean, roll(k, 1))
            shut = ocean * os[lev, near(1)]
            north = un[lev, near(0)] * (shut * TWELFTH), kn[lev, near(0)] * shut
            shut = ocean * os[lev, near(-1)]
            south = un[lev, near(-1)] * (shut * TWELFTH), kn[lev, near(-1)] * shut
            w = weigh(ocean, (u, k), (uw, kw), north, south)
            for n in range(9):
                wt[9 * lev + n, blk] = w[n]
            for t in range(2):
                m = 3 * t + lev
                spot = 32 * g + 4 * m
                sides = roll(both, 126 - spot)
                new = apply(
                    w, q0[m, near(0)], sides, q0[m, near(-2)], q0[m, near(-1)], q0[m, near(1)], q0[m, near(2)], lane
                )
                q1[m, near(0)] = new
                to_e = place(to_e, new, 126, spot, 2, lane)
                to_w = place(to_w, new, 0, spot + 2, 2, lane)
    return to_e, to_w


def inner_kernel(q0, os, un, kn, ue, ke, re_ref, rw_ref, wt, q1, e_ref, w_ref):
    lane = lanes()

    def body(i, carry):
        none = jnp.zeros((8, 128), F32)
        to_e, to_w = advance(i, range(GROUPS), none, none, lane, q0, os, un, kn, ue, ke, re_ref, rw_ref, wt, q1)
        e_ref[tile(i)] = to_e
        w_ref[tile(i)] = to_w
        return carry

    lax.fori_loop(0, BLOCKS, body, 0)


def edge_kernel(
    ue, ke, re_ref, rw_ref, ra_ref, rb_ref, q0_, os_, un_, kn_, wt_, q1_, e_, w_,
    q0, os, un, kn, wt, q1, e_ref, w_ref, hc_ref, hq_ref,
    nh, sh,
):
    lane = lanes()
    lat = lax.axis_index("lat")
    even = lax.rem(lat, 2) == 0
    southern = lat == 0
    northern = lat == lax.axis_size("lat") - 1
    first, second = ra_ref[...], rb_ref[...]
    sh[...] = jnp.where(southern, 0.0, jnp.where(even, second, first))
    nh[...] = jnp.where(even, first, second)

    @pl.when(northern)
    def _():
        f = flip(rb_ref[...])
        shifted = roll(f, -1)
        for m in range(MEM):
            for r in range(4):
                nh[4 * m + r : 4 * m + r + 1] = f[4 * m + 3 - r : 4 * m + 4 - r]
        for lev in range(LEV):
            base = 24 + 12 * lev
            for to, source, x in (
                (0, 1, -f), (1, 0, -f), (2, 2, -f), (3, 4, f), (4, 3, f), (5, 5, f),
                (6, 7, -shifted), (7, 6, -shifted), (8, 9, shifted), (9, 8, shifted), (10, 11, f), (11, 10, f),
            ):
                nh[base + to : base + to + 1] = x[base + source : base + source + 1]

    for m in range(MEM):
        q0[m, 4:8] = sh[4 * m : 4 * m + 4]
        q0[m, 264:268] = nh[4 * m : 4 * m + 4]
    for lev in range(LEV):
        base = 24 + 12 * lev
        top = os[lev, 263:264]
        os[lev, 264:265] = jnp.where(northern, top, nh[base + 10 : base + 11])
        os[lev, 7:8] = sh[base + 11 : base + 12]
        un[lev, 7:8] = sh[base + 2 : base + 3]
        kn[lev, 7:8] = sh[base + 5 : base + 6]
    for i, g in ((0, 0), (BLOCKS - 1, GROUPS - 1)):
        to_e, to_w = advance(
            i, (g,), e_ref[tile(i)], w_ref[tile(i)], lane, q0, os, un, kn, ue, ke, re_ref, rw_ref, wt, q1
        )
        e_ref[tile(i)] = to_e
        w_ref[tile(i)] = to_w

    hc_ref[...] = jnp.zeros((7 * LEV, 8, 128), F32)
    hq_ref[...] = jnp.zeros((5 * MEM, 8, 128), F32)
    for lev in range(LEV):
        base = 24 + 12 * lev
        low = os[lev, 7:8] * os[lev, 8:9]
        high = os[lev, 263:264] * os[lev, 264:265]
        for n, (ref, slot) in enumerate(((un, 0), (kn, 3))):
            lower = jnp.where(northern, nh[base + slot + 2 : base + slot + 3], ref[lev, 263:264] * high)
            hc_ref[7 * lev + n, 0:2] = sh[base + slot : base + slot + 2]
            hc_ref[7 * lev + n, 2:3] = lower
            hc_ref[7 * lev + n, 3:4] = nh[base + slot : base + slot + 1]
            hc_ref[7 * lev + 2 + n, 0:1] = sh[base + slot + 1 : base + slot + 2]
            hc_ref[7 * lev + 2 + n, 1:2] = ref[lev, 7:8] * low
            hc_ref[7 * lev + 2 + n, 2:4] = nh[base + slot : base + slot + 2]
        for n in range(3):
            hc_ref[7 * lev + 4 + n, 0:2] = sh[base + 6 + 2 * n : base + 8 + 2 * n]
            hc_ref[7 * lev + 4 + n, 2:4] = nh[base + 6 + 2 * n : base + 8 + 2 * n]
    for m in range(MEM):
        for k in range(5):
            hq_ref[6 * k + m, 0:2] = q0[m, 4 + k : 6 + k]
            hq_ref[6 * k + m, 2:4] = q0[m, 262 + k : 264 + k]
    to_e = jnp.zeros((8, 128), F32)
    to_w = jnp.zeros((8, 128), F32)
    for m in range(MEM):
        q = hq_ref[12 + m]
        to_e = place(to_e, q, 126, 4 * m, 2, lane)
        to_w = place(to_w, q, 0, 4 * m + 2, 2, lane)
    for lev in range(LEV):
        u, k, ocean = hc_ref[7 * lev + 4], hc_ref[7 * lev + 5], hc_ref[7 * lev + 6]
        for x, spot in ((u, 32), (k, 35), (ocean, 38)):
            to_e = place(to_e, x, 127, spot + lev, 1, lane)
            to_w = place(to_w, x, 0 if spot == 38 else 127, spot + lev, 1, lane)
    e_ref[64:72] = to_e
    w_ref[64:72] = to_w


def last_kernel(wt, hc_ref, hq_ref, re_ref, rw_ref, q1_, out_ref, q1, new_ref, sems):
    lane = lanes()
    row = lax.broadcasted_iota(jnp.int32, (8, 128), 0)
    northern = lax.axis_index("lat") == lax.axis_size("lat") - 1
    folded = (row >= 2) & northern
    from_w, from_e = re_ref[64:72], rw_ref[64:72]
    both = jnp.where((lane & 2) == 0, from_w, from_e)
    for lev in range(LEV):
        ulo, klo, uup, kup, u, k, ocean = (hc_ref[7 * lev + n] for n in range(7))
        ocean_w = roll(from_w, -(38 + lev))
        ocean_e = roll(from_e, 127 - 38 - lev)

        def ends(x, spot, ocean=ocean, ocean_w=ocean_w, ocean_e=ocean_e):
            east = jnp.where(folded, roll(from_e, 127 - spot) * ocean, x * ocean_e)
            west = jnp.where(folded, roll(x, 1) * ocean_w, roll(from_w, -spot) * ocean)
            return jnp.where(lane == 127, east, x), jnp.where(lane == 0, west, roll(x, 1))

        ue, uw = ends(u, 32 + lev)
        ke, kw = ends(k, 35 + lev)
        w = weigh(ocean, (ue * TWELFTH, ke), (uw * TWELFTH, kw), (uup * TWELFTH, kup), (ulo * TWELFTH, klo))
        for t in range(2):
            m = 3 * t + lev
            q = [hq_ref[6 * n + m] for n in range(5)]
            new = apply(w, q[2], roll(both, 126 - 4 * m), q[0], q[1], q[3], q[4], lane)
            q1[m, 6:8] = new[0:2]
            q1[m, 264:266] = new[2:4]

    def body(i, carry):
        both = jnp.where((lane & 2) == 0, re_ref[tile(i)], rw_ref[tile(i)])
        for g in range(GROUPS):
            blk = chunk(i, 8 * g)

            def near(k, g=g):
                return chunk(i, 8 * g + 8 + k)

            for lev in range(LEV):
                w = [wt[9 * lev + n, blk] for n in range(9)]
                for t in range(2):
                    m = 3 * t + lev
                    sides = roll(both, 126 - 32 * g - 4 * m)
                    new_ref[t, lev, blk] = apply(
                        w, q1[m, near(0)], sides, q1[m, near(-2)], q1[m, near(-1)], q1[m, near(1)], q1[m, near(2)], lane
                    )
        return carry

    parts = []
    for n in range(4):
        lax.fori_loop(2 * n, 2 * n + 2, body, 0)
        rows = pl.ds(64 * n, 64)
        part = pltpu.make_async_copy(new_ref.at[:, :, rows], out_ref.at[:, :, rows], sems.at[n])
        part.start()
        parts.append(part)
    for part in parts:
        part.wait()


VMEM = pl.BlockSpec(memory_space=pltpu.VMEM)
HBM = pl.BlockSpec(memory_space=pltpu.HBM)


def call(kernel, name, operands, shapes, scratch=(), inside=VMEM, outside=None, alias=None):
    return pl.pallas_call(
        kernel,
        out_shape=[jax.ShapeDtypeStruct(s, F32) for s in shapes],
        in_specs=[inside] * len(operands),
        out_specs=outside or [VMEM] * len(shapes),
        scratch_shapes=list(scratch),
        input_output_aliases=alias or {},
        compiler_params=pltpu.CompilerParams(vmem_limit_bytes=16 * 2**20),
        name=name,
    )(*operands)


def patterns(height, width):
    def flat(make):
        return [
            (lat * width + lon, (to[0] % height) * width + to[1] % width)
            for lat in range(height)
            for lon in range(width)
            for to in [make(lat, lon)]
        ]

    def odd(pivot):
        def make(lat, lon):
            if lat == height - 1:
                return lat, pivot - 1 - lon
            if lat == 0:
                return lat, lon
            return (lat + 1, lon) if lat % 2 else (lat - 1, lon)

        return flat(make)

    east = flat(lambda lat, lon: (lat, lon + 1))
    west = flat(lambda lat, lon: (lat, lon - 1))
    pairs = flat(lambda lat, lon: (lat + 1, lon) if lat % 2 == 0 else (lat - 1, lon))
    return east, west, pairs, odd


def local(height, width, tracers, east_courant, north_courant, east_kappa, north_kappa, ocean_mask, fold_map):
    east, west, pairs, odd = patterns(height, width)
    fields = (tracers, east_courant, north_courant, east_kappa, north_kappa, ocean_mask)
    pivot = ((fold_map[0] + 1) // 128 + lax.axis_index("lon")) % width
    edge, side = (64, 128), (72, 128)
    ext, own, state = (LEV, ROWS + 16, 128), (LEV, ROWS, 128), (MEM, ROWS + 16, 128)
    a, b, e, w, q0, os, un, kn, ue, ke = call(
        pack_kernel,
        "pack",
        [pltpu.with_memory_space_constraint(x, pltpu.HBM) for x in fields],
        [edge] * 4 + [state, ext, ext, ext, own, own],
        [
            pltpu.VMEM((2, LEV, ROWS, 128), F32),
            pltpu.VMEM((LEV, ROWS, 128), jnp.int32),
            pltpu.VMEM(edge, F32),
            pltpu.VMEM(edge, F32),
            pltpu.SemaphoreType.DMA((6,)),
        ],
        inside=HBM,
    )
    weights = (9 * LEV, ROWS, 128)

    re = lax.ppermute(e, BOTH, east)
    rw = lax.ppermute(w, BOTH, west)
    ra = lax.ppermute(a, BOTH, pairs)
    rb = lax.switch(pivot, [lambda x, p=p: lax.ppermute(x, BOTH, odd(p)) for p in range(width)], b)
    wt, q1, e, w = call(inner_kernel, "inner", (q0, os, un, kn, ue, ke, re, rw), [weights, state, side, side])
    q0, os, un, kn, wt, q1, e, w, hc, hq = call(
        edge_kernel,
        "edge",
        (ue, ke, re, rw, ra, rb, q0, os, un, kn, wt, q1, e, w),
        [state, ext, ext, ext, weights, state, side, side, (7 * LEV, 8, 128), (5 * MEM, 8, 128)],
        [pltpu.VMEM(edge, F32), pltpu.VMEM(edge, F32)],
        alias={6 + n: n for n in range(8)},
    )
    re = lax.ppermute(e, BOTH, east)
    rw = lax.ppermute(w, BOTH, west)
    out, _ = call(
        last_kernel,
        "last",
        (wt, hc, hq, re, rw, q1),
        [(2, LEV, ROWS, 128), state],
        [pltpu.VMEM((2, LEV, ROWS, 128), F32), pltpu.SemaphoreType.DMA((4,))],
        outside=[HBM, VMEM],
        alias={5: 1},
    )
    return out


def solution(mesh):
    plane = P(None, "lat", "lon")
    grid = P(None, None, "lat", "lon")
    return jax.shard_map(
        functools.partial(local, mesh.shape["lat"], mesh.shape["lon"]),
        mesh=mesh,
        in_specs=(grid, plane, plane, plane, plane, plane, P("lon")),
        out_specs=grid,
        check_vma=False,
    )
```

time: 47.5 us -> 35.7 us (0.75); the launches traced: 46.8 us -> 35.5 us
  local copies, waits for them, and re-layouts: 12.2 us -> 0 us
  Pallas kernels: 11.1 us -> 12 us
    unnamed x24 -> x0, local copies, waits for them, and re-layouts: 12.2 us -> none
    pallas_call x3 -> x4, Pallas kernels: 11.1 us -> 12 us  [call(): pl.pallas_call(kernel, out_shape=[jax.ShapeDtypeStruct(s, F32) for s in s...]
  transfers between devices with their start and end apart: 6 -> 6, of which waited for: 2 -> 2; matrix products, arithmetic and copies ran while one was open for 0% -> 0% of each run, Pallas kernels for 0% -> 15%
where the time goes in v2:
time: 35.7 us; the launch traced here: 35.5 us
  starting transfers between devices  15.9 us (45%)
  Pallas kernels  12 us (34%)
  waiting for transfers between devices  6.84 us (19%)
  between operations  0.72 us (2%)
    pallas_call x4, Pallas kernels, call(): pl.pallas_call(kernel, out_shape=[jax.ShapeDtypeStruct(s, F32) for s in s...  12 us
    ppermute x2, starting transfers between devices, local(): rw = lax.ppermute(w, BOTH, west)  9.85 us
    ppermute x1, waiting for transfers between devices, local(): lax.ppermute(x, BOTH, odd(p))  5.19 us
    ppermute x1, starting transfers between devices, local(): lax.ppermute(x, BOTH, odd(p))  4.33 us
    ppermute x2, waiting for transfers between devices, local(): re = lax.ppermute(e, BOTH, east)  1.64 us
    ppermute x1, starting transfers between devices, local(): ra = lax.ppermute(a, BOTH, pairs)  1.58 us
  transfers between devices with their start and end apart: 6, of which 2 were waited for; matrix products, arithmetic and copies ran while one was open for 0% of the time, Pallas kernels for 15%

profile of v2, /device:TPU:4, one launch (start us, length us, event | category | flops | bytes accessed | tf_op | source)
XLA Modules:
  0.0 35.5 jit_solution(14441813320030436901)
XLA Ops:
  0.0 2.7 %pack.1 = (f32[64,128]{1,0:T(8,128)S(1)}, f32[64,128]{1,0:T(8,128)S(1)}, f32[64,128]{1,0:T(8,128)S(1)}, f32[64,128]{1,0:T(8,128)S(1)}, f32[6,272,128]{2,1,0:T(8,...) custom-call(f32[2,3,256,128]{3,2,1,0:T(8,128)} %t_in.1, ...), custom_call_target="tpu_custom_call" | custom-call | tf_op jit(solution)/shard_map/pack/pallas_call | solution.py:360
  2.7 0.1 collective-permute-start.32
  2.8 6.0 %collective-permute-start.33 = (f32[64,128]{1,0:T(8,128)S(1)}, f32[64,128]{1,0:T(8,128)S(1)}, u32[]{:S(2)}, u32[]{:S(2)}) collective-permute-start(f32[64,128]{1,0:T(8,128)S(1)} %get-tuple-element.94), channel_id=1, source_target_pairs={{0,31},{1,0},{2,1},{3,2},{4,3},{5,4},{6,5},{7,6},{8,7},{9,8},{10,9... | collective-permute-start | bytes 98312 | tf_op jit(solution)/shard_map/ppermute | solution.py:420
  8.8 1.6 %collective-permute-start.34 = (f32[64,128]{1,0:T(8,128)S(1)}, f32[64,128]{1,0:T(8,128)S(1)}, u32[]{:S(2)}, u32[]{:S(2)}) collective-permute-start(f32[64,128]{1,0:T(8,128)S(1)} %get-tuple-element.95), channel_id=1, source_target_pairs={{0,32},{1,33},{2,34},{3,35},{4,36},{5,37},{6,38},{7,39},{8,40},{9,... | collective-permute-start | bytes 98312 | tf_op jit(solution)/shard_map/ppermute | solution.py:421
  11.1 9.6 %conditional.1 = (f32[64,128]{1,0:T(8,128)}) conditional(s32[]{:T(128)} %clamp.3, f32[64,128]{1,0:T(8,128)S(1)} %get-tuple-element.96, f32[64,128]{1,0:T(8,128)S(1)} %get-tuple-element.96, f32[64,128]{1,0:T(8,128)S(1)} %get-tuple-element.96, f32[64,128]{1,0:T(8,128)S(1)} %get-tuple-element.96, ...), branch_computations={%region_0.1_spmd, %region_1.2_spmd, %region_2.3_spmd, %region_3.4_... | conditional | bytes 131120 | solution.py:422
  11.1 4.3 %collective-permute-start.17 = (f32[64,128]{1,0:T(8,128)S(1)}, f32[64,128]{1,0:T(8,128)}, u32[]{:S(2)}, u32[]{:S(2)}) collective-permute-start(f32[64,128]{1,0:T(8,128)S(1)} %param.17), channel_id=1, source_target_pairs={{0,0},{1,1},{2,2},{3,3},{4,4},{5,5},{6,6},{7,7},{8,8},{9,9},{10,10... | collective-permute-start | bytes 98312 | tf_op jit(solution)/shard_map/cond/branch_17_fun/ppermute | solution.py:422
  15.5 5.2 %collective-permute-done.17 = f32[64,128]{1,0:T(8,128)} collective-permute-done((f32[64,128]{1,0:T(8,128)S(1)}, f32[64,128]{1,0:T(8,128)}, u32[]{:S(2)}, u32[]{:S(2)}) %collective-permute-start.17) | collective-permute-done | bytes 32800 | tf_op jit(solution)/shard_map/cond/branch_17_fun/ppermute | solution.py:422
  20.7 0.0 collective-permute-done.32.re_ref
  20.7 0.0 collective-permute-done.33.rw_ref
  20.7 5.2 %inner.1 = (f32[27,256,128]{2,1,0:T(8,128)S(1)}, f32[6,272,128]{2,1,0:T(8,128)S(1)}, f32[72,128]{1,0:T(8,128)S(1)}, f32[72,128]{1,0:T(8,128)S(1)}) custom-call(f32[6,272,128]{2,1,0:T(8,128)S(1)} %get-tuple-element.97.q0.q0_, f32[3,272,128]{2,1,0:T(8,128)S(1)} %get-tuple-element.98.os.os_, f32[3,272,128]{2,1,0:T(8,128)S(1)} %get-tuple-element.99.un.un_, ...), custom_call_target="tpu_custom_call" | custom-call | tf_op jit(solution)/shard_map/inner/pallas_call | solution.py:360
  25.9 0.0 collective-permute-done.34.ra_ref
  25.9 1.1 %edge.1 = (f32[6,272,128]{2,1,0:T(8,128)S(1)}, f32[3,272,128]{2,1,0:T(8,128)S(1)}, f32[3,272,128]{2,1,0:T(8,128)S(1)}, f32[3,272,128]{2,1,0:T(8,128)S(1)}, f32[2...) custom-call(f32[3,256,128]{2,1,0:T(8,128)S(1)} %get-tuple-element.91, ...), custom_call_target="tpu_custom_call", output_to_operand_aliasing={{0}: (6, {}), {1}: (7, {}), {2}: (8, {}), {3}: (9, {}), {4}... | custom-call | tf_op jit(solution)/shard_map/edge/pallas_call | solution.py:360
  27.0 0.1 collective-permute-start.35
  27.1 3.8 %collective-permute-start.36 = (f32[72,128]{1,0:T(8,128)S(1)}, f32[72,128]{1,0:T(8,128)S(1)}, u32[]{:S(2)}, u32[]{:S(2)}) collective-permute-start(f32[72,128]{1,0:T(8,128)S(1)} %get-tuple-element.109), channel_id=1, source_target_pairs={{0,31},{1,0},{2,1},{3,2},{4,3},{5,4},{6,5},{7,6},{8,7},{9,8},{10,9... | collective-permute-start | bytes 110600 | tf_op jit(solution)/shard_map/ppermute | solution.py:433
  30.9 1.6 %collective-permute-done.35.re_ref = f32[72,128]{1,0:T(8,128)S(1)} collective-permute-done((f32[72,128]{1,0:T(8,128)S(1)}, f32[72,128]{1,0:T(8,128)S(1)}, u32[]{:S(2)}, u32[]{:S(2)}) %collective-permute-start.35) | collective-permute-done | bytes 36896 | tf_op jit(solution)/shard_map/ppermute | solution.py:432
  32.6 0.0 collective-permute-done.36.rw_ref
  32.6 2.9 %last.1 = (f32[2,3,256,128]{3,2,1,0:T(8,128)}, f32[6,272,128]{2,1,0:T(8,128)S(1)}) custom-call(f32[27,256,128]{2,1,0:T(8,128)S(1)} %get-tuple-element.105.wt, f32[21,8,128]{2,1,0:T(8,128)S(1)} %get-tuple-element.106.hc_ref, f32[30,8,128]{2,1,0:T(8,128)S(1)} %get-tuple-element.107.hq_ref, ...), custom_call_target="tpu_custom_call", output_to_operand_aliasing={{1}: (5, {})} | custom-call | tf_op jit(solution)/shard_map/last/pallas_call | solution.py:360
Async XLA Ops:
  2.7 17.9 %collective-permute-start.32 = (f32[64,128]{1,0:T(8,128)S(1)}, f32[64,128]{1,0:T(8,128)S(1)}, u32[]{:S(2)}, u32[]{:S(2)}) collective-permute-start(f32[64,128]{1,0:T(8,128)S(1)} %get-tuple-element.93), channel_id=1, source_target_pairs={{0,1},{1,2},{2,3},{3,4},{4,5},{5,6},{6,7},{7,8},{8,9},{9,10},{10,1... | collective-permute-start | bytes 98312 | tf_op jit(solution)/shard_map/ppermute | solution.py:419
  2.8 17.8 %collective-permute-start.33 = (f32[64,128]{1,0:T(8,128)S(1)}, f32[64,128]{1,0:T(8,128)S(1)}, u32[]{:S(2)}, u32[]{:S(2)}) collective-permute-start(f32[64,128]{1,0:T(8,128)S(1)} %get-tuple-element.94), channel_id=1, source_target_pairs={{0,31},{1,0},{2,1},{3,2},{4,3},{5,4},{6,5},{7,6},{8,7},{9,8},{10,9... | collective-permute-start | bytes 98312 | tf_op jit(solution)/shard_map/ppermute | solution.py:420
  8.8 17.1 %collective-permute-start.34 = (f32[64,128]{1,0:T(8,128)S(1)}, f32[64,128]{1,0:T(8,128)S(1)}, u32[]{:S(2)}, u32[]{:S(2)}) collective-permute-start(f32[64,128]{1,0:T(8,128)S(1)} %get-tuple-element.95), channel_id=1, source_target_pairs={{0,32},{1,33},{2,34},{3,35},{4,36},{5,37},{6,38},{7,39},{8,40},{9,... | collective-permute-start | bytes 98312 | tf_op jit(solution)/shard_map/ppermute | solution.py:421
  11.1 9.5 %collective-permute-start.17 = (f32[64,128]{1,0:T(8,128)S(1)}, f32[64,128]{1,0:T(8,128)}, u32[]{:S(2)}, u32[]{:S(2)}) collective-permute-start(f32[64,128]{1,0:T(8,128)S(1)} %param.17), channel_id=1, source_target_pairs={{0,0},{1,1},{2,2},{3,3},{4,4},{5,5},{6,6},{7,7},{8,8},{9,9},{10,10... | collective-permute-start | bytes 98312 | tf_op jit(solution)/shard_map/cond/branch_17_fun/ppermute | solution.py:422
  27.0 5.6 %collective-permute-start.35 = (f32[72,128]{1,0:T(8,128)S(1)}, f32[72,128]{1,0:T(8,128)S(1)}, u32[]{:S(2)}, u32[]{:S(2)}) collective-permute-start(f32[72,128]{1,0:T(8,128)S(1)} %get-tuple-element.108), channel_id=1, source_target_pairs={{0,1},{1,2},{2,3},{3,4},{4,5},{5,6},{6,7},{7,8},{8,9},{9,10},{10,1... | collective-permute-start | bytes 110600 | tf_op jit(solution)/shard_map/ppermute | solution.py:432
  27.1 5.5 %collective-permute-start.36 = (f32[72,128]{1,0:T(8,128)S(1)}, f32[72,128]{1,0:T(8,128)S(1)}, u32[]{:S(2)}, u32[]{:S(2)}) collective-permute-start(f32[72,128]{1,0:T(8,128)S(1)} %get-tuple-element.109), channel_id=1, source_target_pairs={{0,31},{1,0},{2,1},{3,2},{4,3},{5,4},{6,5},{7,6},{8,7},{9,8},{10,9... | collective-permute-start | bytes 110600 | tf_op jit(solution)/shard_map/ppermute | solution.py:433

commit v3 on v2

--- a/solution.py
+++ b/solution.py
@@ -85,26 +85,30 @@
     a_ref, b_ref, e_ref, w_ref, q0, os, un, kn, ue, ke,
     tv, mv, nb, sb, sems,
 ):
+    half = ROWS // 2
+    copies = []
+    for n in range(2):
+        rows = pl.ds(half * n, half)
+        for source, target in (
+            (m_in.at[:, rows], mv.at[:, rows]),
+            (t_in.at[:, :, rows], tv.at[:, :, rows]),
+            (ue_in.at[:, rows], ue.at[:, rows]),
+            (ke_in.at[:, rows], ke.at[:, rows]),
+        ):
+            copies.append(pltpu.make_async_copy(source, target, sems.at[len(copies)]))
     own = pl.ds(8, ROWS)
-    copies = [
-        pltpu.make_async_copy(m_in, mv, sems.at[0]),
-        pltpu.make_async_copy(t_in, tv, sems.at[1]),
-        pltpu.make_async_copy(ue_in, ue, sems.at[2]),
-        pltpu.make_async_copy(ke_in, ke, sems.at[3]),
-        pltpu.make_async_copy(un_in, un.at[:, own], sems.at[4]),
-        pltpu.make_async_copy(kn_in, kn.at[:, own], sems.at[5]),
-    ]
+    copies.append(pltpu.make_async_copy(un_in, un.at[:, own], sems.at[8]))
+    copies.append(pltpu.make_async_copy(kn_in, kn.at[:, own], sems.at[9]))
     for c in copies:
         c.start()
     lane = lanes()
     nb[...] = jnp.zeros((64, 128), F32)
     sb[...] = jnp.zeros((64, 128), F32)
-    for c in copies[:4]:
-        c.wait()
 
     def body(i, carry):
         to_e = jnp.zeros((8, 128), F32)
         to_w = jnp.zeros((8, 128), F32)
+        both = jnp.zeros((8, 128), F32)
         for g in range(GROUPS):
             blk, ext = chunk(i, 8 * g), chunk(i, 8 * g + 8)
             for lev in range(LEV):
@@ -118,15 +122,17 @@
                     m = 3 * t + lev
                     q = tv[t, lev, blk] * ocean
                     q0[m, ext] = q
-                    at = 32 * g + 4 * m
-                    to_e = place(to_e, q, 126, at, 2, lane)
-                    to_w = place(to_w, q, 0, at + 2, 2, lane)
-        e_ref[tile(i)] = to_e
-        w_ref[tile(i)] = to_w
+                    both = place(both, q, 126, 32 * g + 4 * m, 4, lane)
+        states = (lane & 31) < 24
+        e_ref[tile(i)] = jnp.where(states, both, to_e)
+        w_ref[tile(i)] = jnp.where(states, both, to_w)
         return carry
 
-    lax.fori_loop(0, BLOCKS, body, 0)
-    for c in copies[4:]:
+    for n in range(2):
+        for c in copies[4 * n : 4 * n + 4]:
+            c.wait()
+        lax.fori_loop(BLOCKS // 2 * n, BLOCKS // 2 * (n + 1), body, 0)
+    for c in copies[8:]:
         c.wait()
     for lev in range(LEV):
         base = 24 + 12 * lev
@@ -157,66 +163,12 @@
 
 
 def flip(x):
-    lane = lax.broadcasted_iota(jnp.int32, x.shape, 1)
-    for s in (1, 2, 4, 8, 16, 32, 64):
-        x = jnp.where((lane & s) != 0, roll(x, s), roll(x, -s))
-    return x
-
-
-def advance(i, groups, to_e, to_w, lane, q0, os, un, kn, ue, ke, re_ref, rw_ref, wt, q1):
-    from_w, from_e = re_ref[tile(i)], rw_ref[tile(i)]
-    both = jnp.where((lane & 2) == 0, from_w, from_e)
-    for g in groups:
-        blk = chunk(i, 8 * g)
-
-        def near(k, g=g):
-            return chunk(i, 8 * g + 8 + k)
-
-        for lev in range(LEV):
-            ocean = os[lev, near(0)]
-            spot = 32 * g + 24 + lev
-            beside = jnp.where(lane == 127, roll(from_e, 127 - spot), roll(ocean, -1))
-            shut = ocean * beside
-            u = ue[lev, blk] * (shut * TWELFTH)
-            k = ke[lev, blk] * shut
-            uw = jnp.where(lane == 0, roll(from_w, -spot) * (ocean * TWELFTH), roll(u, 1))
-            kw = jnp.where(lane == 0, roll(from_w, -(spot + 3)) * ocean, roll(k, 1))
-            shut = ocean * os[lev, near(1)]
-            north = un[lev, near(0)] * (shut * TWELFTH), kn[lev, near(0)] * shut
-            shut = ocean * os[lev, near(-1)]
-            south = un[lev, near(-1)] * (shut * TWELFTH), kn[lev, near(-1)] * shut
-            w = weigh(ocean, (u, k), (uw, kw), north, south)
-            for n in range(9):
-                wt[9 * lev + n, blk] = w[n]
-            for t in range(2):
-                m = 3 * t + lev
-                spot = 32 * g + 4 * m
-                sides = roll(both, 126 - spot)
-                new = apply(
-                    w, q0[m, near(0)], sides, q0[m, near(-2)], q0[m, near(-1)], q0[m, near(1)], q0[m, near(2)], lane
-                )
-                q1[m, near(0)] = new
-                to_e = place(to_e, new, 126, spot, 2, lane)
-                to_w = place(to_w, new, 0, spot + 2, 2, lane)
-    return to_e, to_w
-
-
-def inner_kernel(q0, os, un, kn, ue, ke, re_ref, rw_ref, wt, q1, e_ref, w_ref):
-    lane = lanes()
-
-    def body(i, carry):
-        none = jnp.zeros((8, 128), F32)
-        to_e, to_w = advance(i, range(GROUPS), none, none, lane, q0, os, un, kn, ue, ke, re_ref, rw_ref, wt, q1)
-        e_ref[tile(i)] = to_e
-        w_ref[tile(i)] = to_w
-        return carry
-
-    lax.fori_loop(0, BLOCKS, body, 0)
-
-
-def edge_kernel(
-    ue, ke, re_ref, rw_ref, ra_ref, rb_ref, q0_, os_, un_, kn_, wt_, q1_, e_, w_,
-    q0, os, un, kn, wt, q1, e_ref, w_ref, hc_ref, hq_ref,
+    return jnp.take_along_axis(x, 127 - lax.broadcasted_iota(jnp.int32, x.shape, 1), axis=1)
+
+
+def step_kernel(
+    ue, ke, re_ref, rw_ref, ra_ref, rb_ref, q0_, os_, un_, kn_,
+    q0, os, un, kn, wt, q1, s_ref, hc_ref, hq_ref,
     nh, sh,
 ):
     lane = lanes()
@@ -253,12 +205,59 @@
         os[lev, 7:8] = sh[base + 11 : base + 12]
         un[lev, 7:8] = sh[base + 2 : base + 3]
         kn[lev, 7:8] = sh[base + 5 : base + 6]
-    for i, g in ((0, 0), (BLOCKS - 1, GROUPS - 1)):
-        to_e, to_w = advance(
-            i, (g,), e_ref[tile(i)], w_ref[tile(i)], lane, q0, os, un, kn, ue, ke, re_ref, rw_ref, wt, q1
-        )
-        e_ref[tile(i)] = to_e
-        w_ref[tile(i)] = to_w
+
+    def weights(i, carry):
+        from_w, from_e = re_ref[tile(i)], rw_ref[tile(i)]
+        for g in range(GROUPS):
+            blk = chunk(i, 8 * g)
+
+            def near(k, g=g):
+                return chunk(i, 8 * g + 8 + k)
+
+            for lev in range(LEV):
+                ocean = os[lev, near(0)]
+                spot = 32 * g + 24 + lev
+                beside = jnp.where(lane == 127, roll(from_e, 127 - spot), roll(ocean, -1))
+                shut = ocean * beside
+                u = ue[lev, blk] * (shut * TWELFTH)
+                k = ke[lev, blk] * shut
+                uw = jnp.where(lane == 0, roll(from_w, -spot) * (ocean * TWELFTH), roll(u, 1))
+                kw = jnp.where(lane == 0, roll(from_w, -(spot + 3)) * ocean, roll(k, 1))
+                shut = ocean * os[lev, near(1)]
+                north = un[lev, near(0)] * (shut * TWELFTH), kn[lev, near(0)] * shut
+                shut = ocean * os[lev, near(-1)]
+                south = un[lev, near(-1)] * (shut * TWELFTH), kn[lev, near(-1)] * shut
+                w = weigh(ocean, (u, k), (uw, kw), north, south)
+                for n in range(9):
+                    wt[9 * lev + n, blk] = w[n]
+        return carry
+
+    lax.fori_loop(0, BLOCKS, weights, 0)
+
+    def update(i, carry):
+        both = jnp.where((lane & 2) == 0, re_ref[tile(i)], rw_ref[tile(i)])
+        strip = jnp.zeros((8, 128), F32)
+        for g in range(GROUPS):
+            blk = chunk(i, 8 * g)
+
+            def near(k, g=g):
+                return chunk(i, 8 * g + 8 + k)
+
+            for lev in range(LEV):
+                w = [wt[9 * lev + n, blk] for n in range(9)]
+                for t in range(2):
+                    m = 3 * t + lev
+                    spot = 32 * g + 4 * m
+                    sides = roll(both, 126 - spot)
+                    new = apply(
+                        w, q0[m, near(0)], sides, q0[m, near(-2)], q0[m, near(-1)], q0[m, near(1)], q0[m, near(2)], lane
+                    )
+                    q1[m, near(0)] = new
+                    strip = place(strip, new, 126, spot, 4, lane)
+        s_ref[tile(i)] = strip
+        return carry
+
+    lax.fori_loop(0, BLOCKS, update, 0)
 
     hc_ref[...] = jnp.zeros((7 * LEV, 8, 128), F32)
     hq_ref[...] = jnp.zeros((5 * MEM, 8, 128), F32)
@@ -281,19 +280,15 @@
         for k in range(5):
             hq_ref[6 * k + m, 0:2] = q0[m, 4 + k : 6 + k]
             hq_ref[6 * k + m, 2:4] = q0[m, 262 + k : 264 + k]
-    to_e = jnp.zeros((8, 128), F32)
-    to_w = jnp.zeros((8, 128), F32)
+    strip = jnp.zeros((8, 128), F32)
     for m in range(MEM):
-        q = hq_ref[12 + m]
-        to_e = place(to_e, q, 126, 4 * m, 2, lane)
-        to_w = place(to_w, q, 0, 4 * m + 2, 2, lane)
+        strip = place(strip, hq_ref[12 + m], 126, 4 * m, 4, lane)
     for lev in range(LEV):
         u, k, ocean = hc_ref[7 * lev + 4], hc_ref[7 * lev + 5], hc_ref[7 * lev + 6]
-        for x, spot in ((u, 32), (k, 35), (ocean, 38)):
-            to_e = place(to_e, x, 127, spot + lev, 1, lane)
-            to_w = place(to_w, x, 0 if spot == 38 else 127, spot + lev, 1, lane)
-    e_ref[64:72] = to_e
-    w_ref[64:72] = to_w
+        strip = place(strip, u, 127, 32 + lev, 1, lane)
+        strip = place(strip, k, 127, 35 + lev, 1, lane)
+        strip = place(strip, ocean, 127, 38 + 2 * lev, 2, lane)
+    s_ref[64:72] = strip
 
 
 def last_kernel(wt, hc_ref, hq_ref, re_ref, rw_ref, q1_, out_ref, q1, new_ref, sems):
@@ -305,8 +300,8 @@
     both = jnp.where((lane & 2) == 0, from_w, from_e)
     for lev in range(LEV):
         ulo, klo, uup, kup, u, k, ocean = (hc_ref[7 * lev + n] for n in range(7))
-        ocean_w = roll(from_w, -(38 + lev))
-        ocean_e = roll(from_e, 127 - 38 - lev)
+        ocean_w = roll(from_w, -(38 + 2 * lev))
+        ocean_e = roll(from_e, 127 - 39 - 2 * lev)
 
         def ends(x, spot, ocean=ocean, ocean_w=ocean_w, ocean_e=ocean_e):
             east = jnp.where(folded, roll(from_e, 127 - spot) * ocean, x * ocean_e)
@@ -410,7 +405,7 @@
             pltpu.VMEM((LEV, ROWS, 128), jnp.int32),
             pltpu.VMEM(edge, F32),
             pltpu.VMEM(edge, F32),
-            pltpu.SemaphoreType.DMA((6,)),
+            pltpu.SemaphoreType.DMA((10,)),
         ],
         inside=HBM,
     )
@@ -420,17 +415,16 @@
     rw = lax.ppermute(w, BOTH, west)
     ra = lax.ppermute(a, BOTH, pairs)
     rb = lax.switch(pivot, [lambda x, p=p: lax.ppermute(x, BOTH, odd(p)) for p in range(width)], b)
-    wt, q1, e, w = call(inner_kernel, "inner", (q0, os, un, kn, ue, ke, re, rw), [weights, state, side, side])
-    q0, os, un, kn, wt, q1, e, w, hc, hq = call(
-        edge_kernel,
-        "edge",
-        (ue, ke, re, rw, ra, rb, q0, os, un, kn, wt, q1, e, w),
-        [state, ext, ext, ext, weights, state, side, side, (7 * LEV, 8, 128), (5 * MEM, 8, 128)],
+    q0, os, un, kn, wt, q1, s, hc, hq = call(
+        step_kernel,
+        "step",
+        (ue, ke, re, rw, ra, rb, q0, os, un, kn),
+        [state, ext, ext, ext, weights, state, side, (7 * LEV, 8, 128), (5 * MEM, 8, 128)],
         [pltpu.VMEM(edge, F32), pltpu.VMEM(edge, F32)],
-        alias={6 + n: n for n in range(8)},
+        alias={6 + n: n for n in range(4)},
     )
-    re = lax.ppermute(e, BOTH, east)
-    rw = lax.ppermute(w, BOTH, west)
+    re = lax.ppermute(s, BOTH, east)
+    rw = lax.ppermute(s, BOTH, west)
     out, _ = call(
         last_kernel,
         "last",

time: 35.7 us -> 34.3 us (0.961)
  waiting for transfers between devices: 6.84 us -> 10.3 us
  starting transfers between devices: 15.9 us -> 12.6 us
  Pallas kernels: 12 us -> 10.5 us
    ppermute x0 -> x2, waiting for transfers between devices: none -> 5.07 us  [the longest x1 3.94 us: local(): re = lax.ppermute(s, BOTH, east)]
    ppermute x2 -> x1, starting transfers between devices: 9.85 us -> 6.01 us  [local(): rw = lax.ppermute(w, BOTH, west)]
    ppermute x2 -> x1, waiting for transfers between devices: 1.64 us -> 0.01 us  [local(): re = lax.ppermute(e, BOTH, east)]
    pallas_call x4 -> x3, Pallas kernels: 12 us -> 10.5 us  [call(): pl.pallas_call(kernel, out_shape=[jax.ShapeDtypeStruct(s, F32) for s in s...]
    ppermute x0 -> x2, starting transfers between devices: none -> 0.58 us  [the longest x1 0.5 us: local(): re = lax.ppermute(s, BOTH, east)]
  transfers between devices with their start and end apart: 6 -> 6, of which waited for: 2 -> 3; matrix products, arithmetic and copies ran while one was open for 0% -> 0% of each run, Pallas kernels for 15% -> 0%
where the time goes in v3:
time: 34.3 us; the launch traced here: 34.1 us
  starting transfers between devices  12.6 us (37%)
  Pallas kernels  10.5 us (31%)
  waiting for transfers between devices  10.3 us (30%)
  between operations  0.73 us (2%)
    pallas_call x3, Pallas kernels, call(): pl.pallas_call(kernel, out_shape=[jax.ShapeDtypeStruct(s, F32) for s in s...  10.5 us
    ppermute x1, starting transfers between devices, local(): rw = lax.ppermute(w, BOTH, west)  6.01 us
    ppermute x1, waiting for transfers between devices, local(): lax.ppermute(x, BOTH, odd(p))  5.19 us
    ppermute x1, starting transfers between devices, local(): lax.ppermute(x, BOTH, odd(p))  4.33 us
    ppermute x1, waiting for transfers between devices, local(): re = lax.ppermute(s, BOTH, east)  3.94 us
    ppermute x1, starting transfers between devices, local(): ra = lax.ppermute(a, BOTH, pairs)  1.58 us
    ppermute x1, waiting for transfers between devices, local(): rw = lax.ppermute(s, BOTH, west)  1.13 us
  transfers between devices with their start and end apart: 6, of which 3 were waited for; matrix products, arithmetic and copies ran while one was open for 0% of the time, Pallas kernels for 0%

profile of v3, /device:TPU:4, one launch (start us, length us, event | category | flops | bytes accessed | tf_op | source)
XLA Modules:
  0.0 34.1 jit_solution(9503613629981542160)
XLA Ops:
  0.0 2.5 %pack.1 = (f32[64,128]{1,0:T(8,128)S(1)}, f32[64,128]{1,0:T(8,128)S(1)}, f32[64,128]{1,0:T(8,128)S(1)}, f32[64,128]{1,0:T(8,128)S(1)}, f32[6,272,128]{2,1,0:T(8,...) custom-call(f32[2,3,256,128]{3,2,1,0:T(8,128)} %t_in.1, ...), custom_call_target="tpu_custom_call" | custom-call | tf_op jit(solution)/shard_map/pack/pallas_call | solution.py:355
  2.5 0.1 collective-permute-start.32
  2.6 6.0 %collective-permute-start.33 = (f32[64,128]{1,0:T(8,128)S(1)}, f32[64,128]{1,0:T(8,128)S(1)}, u32[]{:S(2)}, u32[]{:S(2)}) collective-permute-start(f32[64,128]{1,0:T(8,128)S(1)} %get-tuple-element.89), channel_id=1, source_target_pairs={{0,31},{1,0},{2,1},{3,2},{4,3},{5,4},{6,5},{7,6},{8,7},{9,8},{10,9... | collective-permute-start | bytes 98312 | tf_op jit(solution)/shard_map/ppermute | solution.py:415
  8.6 1.6 %collective-permute-start.34 = (f32[64,128]{1,0:T(8,128)S(1)}, f32[64,128]{1,0:T(8,128)S(1)}, u32[]{:S(2)}, u32[]{:S(2)}) collective-permute-start(f32[64,128]{1,0:T(8,128)S(1)} %get-tuple-element.90), channel_id=1, source_target_pairs={{0,32},{1,33},{2,34},{3,35},{4,36},{5,37},{6,38},{7,39},{8,40},{9,... | collective-permute-start | bytes 98312 | tf_op jit(solution)/shard_map/ppermute | solution.py:416
  10.9 9.6 %conditional.1 = (f32[64,128]{1,0:T(8,128)}) conditional(s32[]{:T(128)} %clamp.3, f32[64,128]{1,0:T(8,128)S(1)} %get-tuple-element.91, f32[64,128]{1,0:T(8,128)S(1)} %get-tuple-element.91, f32[64,128]{1,0:T(8,128)S(1)} %get-tuple-element.91, f32[64,128]{1,0:T(8,128)S(1)} %get-tuple-element.91, ...), branch_computations={%region_0.1_spmd, %region_1.2_spmd, %region_2.3_spmd, %region_3.4_... | conditional | bytes 131120 | solution.py:417
  10.9 4.3 %collective-permute-start.24 = (f32[64,128]{1,0:T(8,128)S(1)}, f32[64,128]{1,0:T(8,128)}, u32[]{:S(2)}, u32[]{:S(2)}) collective-permute-start(f32[64,128]{1,0:T(8,128)S(1)} %param.24), channel_id=1, source_target_pairs={{0,0},{1,1},{2,2},{3,3},{4,4},{5,5},{6,6},{7,7},{8,8},{9,9},{10,10... | collective-permute-start | bytes 98312 | tf_op jit(solution)/shard_map/cond/branch_24_fun/ppermute | solution.py:417
  15.2 5.2 %collective-permute-done.24 = f32[64,128]{1,0:T(8,128)} collective-permute-done((f32[64,128]{1,0:T(8,128)S(1)}, f32[64,128]{1,0:T(8,128)}, u32[]{:S(2)}, u32[]{:S(2)}) %collective-permute-start.24) | collective-permute-done | bytes 32800 | tf_op jit(solution)/shard_map/cond/branch_24_fun/ppermute | solution.py:417
  20.4 0.0 collective-permute-done.32.re_ref
  20.4 0.0 collective-permute-done.33.rw_ref
  20.4 0.0 collective-permute-done.34.ra_ref
  20.4 5.0 %step.1 = (f32[6,272,128]{2,1,0:T(8,128)S(1)}, f32[3,272,128]{2,1,0:T(8,128)S(1)}, f32[3,272,128]{2,1,0:T(8,128)S(1)}, f32[3,272,128]{2,1,0:T(8,128)S(1)}, f32[2...) custom-call(f32[3,256,128]{2,1,0:T(8,128)S(1)} %get-tuple-element.86, ...), custom_call_target="tpu_custom_call", output_to_operand_aliasing={{0}: (6, {}), {1}: (7, {}), {2}: (8, {}), {3}: (9, {})} | custom-call | tf_op jit(solution)/shard_map/step/pallas_call | solution.py:355
  25.5 0.1 collective-permute-start.36
  25.6 0.5 %collective-permute-start.35 = (f32[72,128]{1,0:T(8,128)S(1)}, f32[72,128]{1,0:T(8,128)S(1)}, u32[]{:S(2)}, u32[]{:S(2)}) collective-permute-start(f32[72,128]{1,0:T(8,128)S(1)} %get-tuple-element.99), channel_id=1, source_target_pairs={{0,1},{1,2},{2,3},{3,4},{4,5},{5,6},{6,7},{7,8},{8,9},{9,10},{10,1... | collective-permute-start | bytes 110600 | tf_op jit(solution)/shard_map/ppermute | solution.py:426
  26.1 1.1 %collective-permute-done.36.rw_ref = f32[72,128]{1,0:T(8,128)S(1)} collective-permute-done((f32[72,128]{1,0:T(8,128)S(1)}, f32[72,128]{1,0:T(8,128)S(1)}, u32[]{:S(2)}, u32[]{:S(2)}) %collective-permute-start.36) | collective-permute-done | bytes 36896 | tf_op jit(solution)/shard_map/ppermute | solution.py:427
  27.2 3.9 %collective-permute-done.35.re_ref = f32[72,128]{1,0:T(8,128)S(1)} collective-permute-done((f32[72,128]{1,0:T(8,128)S(1)}, f32[72,128]{1,0:T(8,128)S(1)}, u32[]{:S(2)}, u32[]{:S(2)}) %collective-permute-start.35) | collective-permute-done | bytes 36896 | tf_op jit(solution)/shard_map/ppermute | solution.py:426
  31.1 3.0 %last.1 = (f32[2,3,256,128]{3,2,1,0:T(8,128)}, f32[6,272,128]{2,1,0:T(8,128)S(1)}) custom-call(f32[27,256,128]{2,1,0:T(8,128)S(1)} %get-tuple-element.96.wt, f32[21,8,128]{2,1,0:T(8,128)S(1)} %get-tuple-element.97.hc_ref, f32[30,8,128]{2,1,0:T(8,128)S(1)} %get-tuple-element.98.hq_ref, ...), custom_call_target="tpu_custom_call", output_to_operand_aliasing={{1}: (5, {})} | custom-call | tf_op jit(solution)/shard_map/last/pallas_call | solution.py:355
Async XLA Ops:
  2.5 17.9 %collective-permute-start.32 = (f32[64,128]{1,0:T(8,128)S(1)}, f32[64,128]{1,0:T(8,128)S(1)}, u32[]{:S(2)}, u32[]{:S(2)}) collective-permute-start(f32[64,128]{1,0:T(8,128)S(1)} %get-tuple-element.88), channel_id=1, source_target_pairs={{0,1},{1,2},{2,3},{3,4},{4,5},{5,6},{6,7},{7,8},{8,9},{9,10},{10,1... | collective-permute-start | bytes 98312 | tf_op jit(solution)/shard_map/ppermute | solution.py:414
  2.6 17.8 %collective-permute-start.33 = (f32[64,128]{1,0:T(8,128)S(1)}, f32[64,128]{1,0:T(8,128)S(1)}, u32[]{:S(2)}, u32[]{:S(2)}) collective-permute-start(f32[64,128]{1,0:T(8,128)S(1)} %get-tuple-element.89), channel_id=1, source_target_pairs={{0,31},{1,0},{2,1},{3,2},{4,3},{5,4},{6,5},{7,6},{8,7},{9,8},{10,9... | collective-permute-start | bytes 98312 | tf_op jit(solution)/shard_map/ppermute | solution.py:415
  8.6 11.8 %collective-permute-start.34 = (f32[64,128]{1,0:T(8,128)S(1)}, f32[64,128]{1,0:T(8,128)S(1)}, u32[]{:S(2)}, u32[]{:S(2)}) collective-permute-start(f32[64,128]{1,0:T(8,128)S(1)} %get-tuple-element.90), channel_id=1, source_target_pairs={{0,32},{1,33},{2,34},{3,35},{4,36},{5,37},{6,38},{7,39},{8,40},{9,... | collective-permute-start | bytes 98312 | tf_op jit(solution)/shard_map/ppermute | solution.py:416
  10.9 9.5 %collective-permute-start.24 = (f32[64,128]{1,0:T(8,128)S(1)}, f32[64,128]{1,0:T(8,128)}, u32[]{:S(2)}, u32[]{:S(2)}) collective-permute-start(f32[64,128]{1,0:T(8,128)S(1)} %param.24), channel_id=1, source_target_pairs={{0,0},{1,1},{2,2},{3,3},{4,4},{5,5},{6,6},{7,7},{8,8},{9,9},{10,10... | collective-permute-start | bytes 98312 | tf_op jit(solution)/shard_map/cond/branch_24_fun/ppermute | solution.py:417
  25.5 1.7 %collective-permute-start.36 = (f32[72,128]{1,0:T(8,128)S(1)}, f32[72,128]{1,0:T(8,128)S(1)}, u32[]{:S(2)}, u32[]{:S(2)}) collective-permute-start(f32[72,128]{1,0:T(8,128)S(1)} %get-tuple-element.99), channel_id=1, source_target_pairs={{0,31},{1,0},{2,1},{3,2},{4,3},{5,4},{6,5},{7,6},{8,7},{9,8},{10,9... | collective-permute-start | bytes 110600 | tf_op jit(solution)/shard_map/ppermute | solution.py:427
  25.6 5.6 %collective-permute-start.35 = (f32[72,128]{1,0:T(8,128)S(1)}, f32[72,128]{1,0:T(8,128)S(1)}, u32[]{:S(2)}, u32[]{:S(2)}) collective-permute-start(f32[72,128]{1,0:T(8,128)S(1)} %get-tuple-element.99), channel_id=1, source_target_pairs={{0,1},{1,2},{2,3},{3,4},{4,5},{5,6},{6,7},{7,8},{8,9},{9,10},{10,1... | collective-permute-start | bytes 110600 | tf_op jit(solution)/shard_map/ppermute | solution.py:426
